TPU v7x, 32 devices: a whole 2x2x4 slice. The times are simulated.
32 devices in a mesh: gx: 4 (over y, core), gy: 4 (over z), src: 2 (over x).
Axes of the slice: x: 2, y: 2, z: 4, core: 2. Of those that a mesh axis runs over, the one named last changes fastest.
Arguments:
- conductivity: float32 [8, 32, 128], P('gx', 'gy'), may hold values from 0.3 to 3
- electrodes: int32 [128, 2], replicated, may hold values from 0 to 32767
- pair_order: int32 [128], P('src'), may hold values from 0 to 127, each once
- initial_fields: float32 [128, 8, 32, 128], P('src', 'gx', 'gy'), as said below
- adjoint_fields: float32 [128, 8, 32, 128], P('src', 'gx', 'gy'), may hold values from -6 to 6
Outputs:
- potentials: float32 [128, 8, 32, 128], P('src', 'gx', 'gy')
- gradient: float32 [8, 32, 128], P('gx', 'gy', 'src')
Inputs may be any that keep to these rules, and one draw needn't show every extreme that they name: `electrodes`: flat cell index (x * 32 + y) * 128 + z. `pair_order`: each pair appears once. `initial_fields`: every entry lies within 6 / sqrt(32768) in magnitude.
All inputs are finite; a program needn't handle non-finite values.
Results may differ from a plain program's by a relative error of at most 0.00029.
Values sent between devices are 32-bit elements; how exact they have to be, the bound alone decides.
A program may use at most 64 MiB of HBM per device.

v0:
```python
import jax
import jax.numpy as jnp
from jax import lax
from jax.sharding import PartitionSpec as P

ITERS = 2


INJECT = 4.0


def padded_2(block, sides, width):
    for axis, dim in sides:
        count = lax.axis_size(axis)
        forward = [(i, i + 1) for i in range(count - 1)]
        backward = [(target, source) for source, target in forward]
        low = lax.ppermute(
            lax.slice_in_dim(block, block.shape[dim] - width, None, axis=dim), axis, forward
        )
        high = lax.ppermute(lax.slice_in_dim(block, 0, width, axis=dim), axis, backward)
        block = jnp.concatenate([low, block, high], axis=dim)
    return block


def shifted(x, axis, by):
    length = lax.axis_size(axis)
    pairs = [(i, i + by) for i in range(length) if 0 <= i + by < length]
    return lax.ppermute(x, axis, pairs)


def conductances(sig_pad):
    full = jnp.pad(sig_pad, ((0, 0), (0, 0), (1, 1)))
    cond_x = 0.5 * (full[1:, 1:-1, 1:-1] + full[:-1, 1:-1, 1:-1])
    cond_y = 0.5 * (full[1:-1, 1:, 1:-1] + full[1:-1, :-1, 1:-1])
    cond_z = 0.5 * (full[1:-1, 1:-1, 1:] + full[1:-1, 1:-1, :-1])
    return (cond_x, cond_y, cond_z)


def operator(padded, conds):
    full = jnp.pad(padded, ((0, 0), (0, 0), (0, 0), (1, 1)))
    flux_x = conds[0] * (full[:, 1:, 1:-1, 1:-1] - full[:, :-1, 1:-1, 1:-1])
    flux_y = conds[1] * (full[:, 1:-1, 1:, 1:-1] - full[:, 1:-1, :-1, 1:-1])
    flux_z = conds[2] * (full[:, 1:-1, 1:-1, 1:] - full[:, 1:-1, 1:-1, :-1])
    return (
        flux_x[:, :-1]
        - flux_x[:, 1:]
        + (flux_y[:, :, :-1] - flux_y[:, :, 1:])
        + (flux_z[..., :-1] - flux_z[..., 1:])
    )


def gram_of(left, right):
    return jnp.einsum("axyz,bxyz->ab", left, right, precision=lax.Precision.HIGHEST)


def combine_cols(field, matrix):
    return jnp.einsum("axyz,ab->bxyz", field, matrix, precision=lax.Precision.HIGHEST)


def posdef_solve(matrix, right):
    lower = jnp.linalg.cholesky(matrix)
    middle = lax.linalg.triangular_solve(lower, right, left_side=True, lower=True)
    return lax.linalg.triangular_solve(lower, middle, left_side=True, lower=True, transpose_a=True)


def one_hot(cells, start, count):
    return (cells[:, None] == start + jnp.arange(count, dtype=jnp.int32)[None, :]).astype(
        jnp.float32
    )


def face_terms(field_pad, adjoint_pad):
    fu = jnp.pad(field_pad, ((0, 0), (0, 0), (0, 0), (1, 1)))
    fl = jnp.pad(adjoint_pad, ((0, 0), (0, 0), (0, 0), (1, 1)))
    term_x = jnp.sum(
        (fu[:, 1:, 1:-1, 1:-1] - fu[:, :-1, 1:-1, 1:-1])
        * (fl[:, 1:, 1:-1, 1:-1] - fl[:, :-1, 1:-1, 1:-1]),
        axis=0,
    )
    term_y = jnp.sum(
        (fu[:, 1:-1, 1:, 1:-1] - fu[:, 1:-1, :-1, 1:-1])
        * (fl[:, 1:-1, 1:, 1:-1] - fl[:, 1:-1, :-1, 1:-1]),
        axis=0,
    )
    term_z = jnp.sum(
        (fu[:, 1:-1, 1:-1, 1:] - fu[:, 1:-1, 1:-1, :-1])
        * (fl[:, 1:-1, 1:-1, 1:] - fl[:, 1:-1, 1:-1, :-1]),
        axis=0,
    )
    return (term_x, term_y, term_z)


def on_device(conductivity, electrodes, pair_order, initial_fields, adjoint_fields):
    cells_x, cells_y, cells_z = conductivity.shape
    columns = initial_fields.shape[0]
    total_y = lax.axis_size("gy") * cells_y
    start_x = lax.axis_index("gx") * cells_x
    start_y = lax.axis_index("gy") * cells_y
    picked = jnp.take(electrodes, pair_order, axis=0)

    def point_source(flat):
        xs = flat // (total_y * cells_z)
        ys = flat // cells_z % total_y
        zs = flat % cells_z
        return jnp.einsum(
            "cx,cy,cz->cxyz",
            one_hot(xs, start_x, cells_x),
            one_hot(ys, start_y, cells_y),
            one_hot(zs, 0, cells_z),
        )

    right = INJECT * (point_source(picked[:, 0]) - point_source(picked[:, 1]))
    stacked = jnp.concatenate([conductivity[None], initial_fields], axis=0)
    padded = padded_2(stacked, (("gx", 1), ("gy", 2)), 1)
    conds = conductances(padded[0])
    iterate = initial_fields
    iter_pad = padded[1:]
    residual = right - operator(iter_pad, conds)
    direction = residual
    res_gram = lax.psum(gram_of(residual, residual), ("gx", "gy"))
    for iteration in range(ITERS):
        dir_pad = padded_2(direction, (("gx", 1), ("gy", 2)), 1)
        image = operator(dir_pad, conds)
        curv_gram = lax.psum(gram_of(direction, image), ("gx", "gy"))
        step_mat = posdef_solve(curv_gram, res_gram)
        iterate = iterate + combine_cols(direction, step_mat)
        residual = residual - combine_cols(image, step_mat)
        if iteration + 1 < ITERS:
            new_gram = lax.psum(gram_of(residual, residual), ("gx", "gy"))
            turn_mat = posdef_solve(res_gram, new_gram)
            direction = residual + combine_cols(direction, turn_mat)
            res_gram = new_gram
    field_pad = jnp.pad(iterate, ((0, 0), (1, 1), (1, 1), (0, 0)))
    adj_local = jnp.pad(adjoint_fields, ((0, 0), (1, 1), (1, 1), (0, 0)))
    term_x, term_y, term_z = face_terms(field_pad, adj_local)
    layer_x = jnp.concatenate([iterate[:, :1], adjoint_fields[:, :1]], axis=0)
    layer_y = jnp.concatenate([iterate[:, :, :1], adjoint_fields[:, :, :1]], axis=0)
    after_x = shifted(layer_x, "gx", -1)
    after_y = shifted(layer_y, "gy", -1)
    upper_x = jnp.sum(
        (after_x[:columns, 0] - iterate[:, -1]) * (after_x[columns:, 0] - adjoint_fields[:, -1]),
        axis=0,
    )
    upper_y = jnp.sum(
        (after_y[:columns, :, 0] - iterate[:, :, -1])
        * (after_y[columns:, :, 0] - adjoint_fields[:, :, -1]),
        axis=0,
    )
    lower_x = shifted(upper_x, "gx", 1)
    lower_y = shifted(upper_y, "gy", 1)
    lower_x = jnp.where(lax.axis_index("gx") == 0, term_x[0], lower_x)
    lower_y = jnp.where(lax.axis_index("gy") == 0, term_y[:, 0], lower_y)
    term_x = jnp.concatenate([lower_x[None], term_x[1:-1], upper_x[None]], axis=0)
    term_y = jnp.concatenate([lower_y[:, None], term_y[:, 1:-1], upper_y[:, None]], axis=1)
    local_grad = (
        -0.5
        / columns
        * (
            term_x[:-1]
            + term_x[1:]
            + term_y[:, :-1]
            + term_y[:, 1:]
            + term_z[..., :-1]
            + term_z[..., 1:]
        )
    )
    share = cells_z // lax.axis_size("src")
    summed = lax.psum(local_grad, "src")
    gradient = lax.dynamic_slice_in_dim(summed, lax.axis_index("src") * share, share, 2)
    return (iterate, gradient)


def solution(mesh):
    placed = (
        P("gx", "gy", None),
        P(),
        P("src"),
        P("src", "gx", "gy", None),
        P("src", "gx", "gy", None),
    )
    return jax.shard_map(
        on_device,
        mesh=mesh,
        in_specs=placed,
        out_specs=(P("src", "gx", "gy", None), P("gx", "gy", "src")),
        check_vma=False,
    )
```

profile of v0, /device:TPU:0, one launch (start us, length us, event | category | flops | bytes accessed | tf_op | source)
XLA Modules:
  0.0 304.4 jit_solution(4903056456936579523)
XLA Ops:
  0.6 1.2 copy.88
  2.6 1.3 collective-permute-start.1
  3.9 3.0 %collective-permute-start = (f32[65,1,8,128]{3,0,2,1:T(8,128)S(1)}, f32[65,1,8,128]{3,0,2,1:T(8,128)S(1)}, u32[]{:S(2)}, u32[]{:S(2)}) collective-permute-start(f32[65,1,8,128]{3,0,2,1:T(8,128)S(1)} %get-tuple-element.30), channel_id=1, source_target_pairs={{0,8},{8,16},{16,24},{1,9},{9,17},{17,25},{2,10},{10,18},{18,26},{... | collective-permute-start | bytes 798728 | tf_op jit(solution)/shard_map/ppermute | solution.py:17
  10.4 1.3 collective-permute-start.3
  11.7 5.6 %collective-permute-start.2 = (f32[65,4,1,128]{3,0,2,1:T(8,128)S(1)}, f32[65,4,1,128]{3,0,2,1:T(8,128)S(1)}, u32[]{:S(2)}, u32[]{:S(2)}) collective-permute-start(f32[65,4,1,128]{3,0,2,1:T(8,128)S(1)} %get-tuple-element.24), channel_id=1, source_target_pairs={{0,2},{2,4},{4,6},{1,3},{3,5},{5,7},{8,10},{10,12},{12,14},{9,11},... | collective-permute-start | bytes 399368 | tf_op jit(solution)/shard_map/ppermute | solution.py:17
  17.3 2.0 collective-permute-done.3
  19.3 1.8 collective-permute-done.2
  23.2 1.3 collective-permute-start.4
  24.5 3.1 %collective-permute-start.5 = (f32[64,1,8,128]{3,0,2,1:T(8,128)S(1)}, f32[64,1,8,128]{3,0,2,1:T(8,128)S(1)}, u32[]{:S(2)}, u32[]{:S(2)}) collective-permute-start(f32[64,1,8,128]{3,0,2,1:T(8,128)S(1)} %get-tuple-element.34), channel_id=1, source_target_pairs={{0,8},{8,16},{16,24},{1,9},{9,17},{17,25},{2,10},{10,18},{18,26},{... | collective-permute-start | bytes 786440 | tf_op jit(solution)/shard_map/ppermute | solution.py:17
  28.7 1.3 collective-permute-start.6
  30.0 5.0 %collective-permute-start.7 = (f32[64,4,1,128]{3,0,2,1:T(8,128)S(1)}, f32[64,4,1,128]{3,0,2,1:T(8,128)S(1)}, u32[]{:S(2)}, u32[]{:S(2)}) collective-permute-start(f32[64,4,1,128]{3,0,2,1:T(8,128)S(1)} %get-tuple-element.28), channel_id=1, source_target_pairs={{0,2},{2,4},{4,6},{1,3},{3,5},{5,7},{8,10},{10,12},{12,14},{9,11},... | collective-permute-start | bytes 393224 | tf_op jit(solution)/shard_map/ppermute | solution.py:17
  36.0 1.5 collective-permute-done.7
  39.5 63.8 %all-reduce.8 = (f32[64,64]{0,1:T(8,128)S(1)}, f32[64,64]{0,1:T(8,128)S(1)}) all-reduce(f32[64,64]{0,1:T(8,128)S(1)} %convolution_bitcast_fusion.5, f32[64,64]{0,1:T(8,128)S(1)} %convolution_bitcast_fusion.6), channel_id=1, replica_groups=mesh['gx'=4,'gy'=4,'src'=2] {'gx','gy'}, use_global_device_ids=true, to_apply=%region_3.5 | all-reduce | flops 8192 | bytes 65536 | tf_op jit(solution)/shard_map/psum | solution.py:120
  103.4 5.8 %cholesky.59 = f32[64,64]{1,0:T(8,128)S(1)} custom-call(f32[64,64]{1,0:T(8,128)S(1)} %fusion.67), custom_call_target="Cholesky" | custom-call | tf_op jit(solution)/shard_map/jit(cholesky)/cholesky | solution.py:61
  110.6 4.9 %custom-call.13 = f32[1,64,64]{1,2,0:T(8,128)S(1)} custom-call(f32[1,64,64]{2,1,0:T(8,128)S(1)} %fusion.43), custom_call_target="InvertDiagBlocksLowerTriangular" | custom-call | tf_op jit(solution)/shard_map/triangular_solve/custom-call.2 | solution.py:63
  117.2 58.1 %psum.37 = f32[64,64]{1,0:T(8,128)S(1)} all-reduce(f32[64,64]{1,0:T(8,128)S(1)} %convolution_bitcast_fusion.3), channel_id=1, replica_groups=mesh['gx'=4,'gy'=4,'src'=2] {'gx','gy'}, use_global_device_ids=true, to_apply=%region_4.8 | all-reduce | flops 4096 | bytes 32768 | tf_op jit(solution)/shard_map/psum | solution.py:129
  175.4 5.8 %cholesky.70 = f32[64,64]{1,0:T(8,128)S(1)} custom-call(f32[64,64]{1,0:T(8,128)S(1)} %fusion.63), custom_call_target="Cholesky" | custom-call | tf_op jit(solution)/shard_map/jit(cholesky)/cholesky | solution.py:61
  182.6 4.9 %custom-call.15 = f32[1,64,64]{1,2,0:T(8,128)S(1)} custom-call(f32[1,64,64]{2,1,0:T(8,128)S(1)} %fusion.44), custom_call_target="InvertDiagBlocksLowerTriangular" | custom-call | tf_op jit(solution)/shard_map/triangular_solve/custom-call.2 | solution.py:63
  188.6 1.3 collective-permute-start.8
  189.9 3.0 %collective-permute-start.9 = (f32[64,1,8,128]{3,0,2,1:T(8,128)S(1)}, f32[64,1,8,128]{3,0,2,1:T(8,128)S(1)}, u32[]{:S(2)}, u32[]{:S(2)}) collective-permute-start(f32[64,1,8,128]{3,0,2,1:T(8,128)S(1)} %get-tuple-element.32), channel_id=1, source_target_pairs={{0,8},{8,16},{16,24},{1,9},{9,17},{17,25},{2,10},{10,18},{18,26},{... | collective-permute-start | bytes 786440 | tf_op jit(solution)/shard_map/ppermute | solution.py:17
  194.1 1.3 collective-permute-start.10
  195.4 4.6 %collective-permute-start.11 = (f32[64,4,1,128]{3,0,2,1:T(8,128)S(1)}, f32[64,4,1,128]{3,0,2,1:T(8,128)S(1)}, u32[]{:S(2)}, u32[]{:S(2)}) collective-permute-start(f32[64,4,1,128]{3,0,2,1:T(8,128)S(1)} %get-tuple-element.26), channel_id=1, source_target_pairs={{0,2},{2,4},{4,6},{1,3},{3,5},{5,7},{8,10},{10,12},{12,14},{9,11},... | collective-permute-start | bytes 393224 | tf_op jit(solution)/shard_map/ppermute | solution.py:17
  201.0 1.5 collective-permute-done.11
  204.4 61.2 %psum.38 = f32[64,64]{0,1:T(8,128)S(1)} all-reduce(f32[64,64]{0,1:T(8,128)S(1)} %convolution_bitcast_fusion.1), channel_id=1, replica_groups=mesh['gx'=4,'gy'=4,'src'=2] {'gx','gy'}, use_global_device_ids=true, to_apply=%region_5.9 | all-reduce | flops 4096 | bytes 32768 | tf_op jit(solution)/shard_map/psum | solution.py:124
  265.7 5.8 %cholesky.81 = f32[64,64]{1,0:T(8,128)S(1)} custom-call(f32[64,64]{1,0:T(8,128)S(1)} %fusion.59), custom_call_target="Cholesky" | custom-call | tf_op jit(solution)/shard_map/jit(cholesky)/cholesky | solution.py:61
  272.9 4.9 %custom-call.17 = f32[1,64,64]{1,2,0:T(8,128)S(1)} custom-call(f32[1,64,64]{2,1,0:T(8,128)S(1)} %fusion.45), custom_call_target="InvertDiagBlocksLowerTriangular" | custom-call | tf_op jit(solution)/shard_map/triangular_solve/custom-call.2 | solution.py:63
  279.8 1.4 collective-permute-start.12
  282.6 1.3 collective-permute-start.14
  284.8 5.9 %collective-permute-done.14 = f32[128,2,1,128]{3,0,2,1:T(8,128)S(1)} collective-permute-done((f32[128,2,1,128]{3,0,2,1:T(8,128)S(1)}, f32[128,2,1,128]{3,0,2,1:T(8,128)S(1)}, u32[]{:S(2)}, u32[]{:S(2)}) %collective-permute-start.14) | collective-permute-done | bytes 131104 | tf_op jit(solution)/shard_map/ppermute | solution.py:28
  290.8 1.4 collective-permute-start.15
  292.3 5.6 %collective-permute-start.13 = (f32[8,128]{1,0:T(8,128)S(1)}, f32[8,128]{1,0:T(8,128)S(1)}, u32[]{:S(2)}, u32[]{:S(2)}) collective-permute-start(f32[8,128]{1,0:T(8,128)S(1)} %fusion.40), channel_id=1, source_target_pairs={{0,8},{8,16},{16,24},{1,9},{9,17},{17,25},{2,10},{10,18},{18,26},{... | collective-permute-start | bytes 12296 | tf_op jit(solution)/shard_map/ppermute | solution.py:28
  298.8 5.0 %psum.39 = f32[2,8,128]{2,1,0:T(8,128)S(1)} all-reduce(f32[2,8,128]{2,1,0:T(8,128)S(1)} %fusion.78), channel_id=1, replica_groups=mesh['gx'=4,'gy'=4,'src'=2] {'src'}, use_global_device_ids=true, to_apply=%region_11.15 | all-reduce | flops 2048 | bytes 16384 | tf_op jit(solution)/shard_map/psum | solution.py:168
  (116 shorter events, 27.0 us)
Async XLA Ops:
  0.6 9.8 %copy-start.4 = (f32[2,8,128]{2,1,0:T(8,128)S(1)}, f32[2,8,128]{2,1,0:T(8,128)}, u32[]{:S(2)}) copy-start(f32[2,8,128]{2,1,0:T(8,128)} %param.10) | copy-start | bytes 24580
  2.6 7.8 %collective-permute-start.1 = (f32[65,1,8,128]{3,0,2,1:T(8,128)S(1)}, f32[65,1,8,128]{3,0,2,1:T(8,128)S(1)}, u32[]{:S(2)}, u32[]{:S(2)}) collective-permute-start(f32[65,1,8,128]{3,0,2,1:T(8,128)S(1)} %get-tuple-element.31), channel_id=1, source_target_pairs={{8,0},{16,8},{24,16},{9,1},{17,9},{25,17},{10,2},{18,10},{26,18},{... | collective-permute-start | bytes 798728 | tf_op jit(solution)/shard_map/ppermute | solution.py:20
  3.9 6.5 %collective-permute-start = (f32[65,1,8,128]{3,0,2,1:T(8,128)S(1)}, f32[65,1,8,128]{3,0,2,1:T(8,128)S(1)}, u32[]{:S(2)}, u32[]{:S(2)}) collective-permute-start(f32[65,1,8,128]{3,0,2,1:T(8,128)S(1)} %get-tuple-element.30), channel_id=1, source_target_pairs={{0,8},{8,16},{16,24},{1,9},{9,17},{17,25},{2,10},{10,18},{18,26},{... | collective-permute-start | bytes 798728 | tf_op jit(solution)/shard_map/ppermute | solution.py:17
  10.4 8.9 %collective-permute-start.3 = (f32[65,4,1,128]{3,0,2,1:T(8,128)S(1)}, f32[65,4,1,128]{3,0,2,1:T(8,128)S(1)}, u32[]{:S(2)}, u32[]{:S(2)}) collective-permute-start(f32[65,4,1,128]{3,0,2,1:T(8,128)S(1)} %get-tuple-element.25), channel_id=1, source_target_pairs={{2,0},{4,2},{6,4},{3,1},{5,3},{7,5},{10,8},{12,10},{14,12},{11,9},... | collective-permute-start | bytes 399368 | tf_op jit(solution)/shard_map/ppermute | solution.py:20
  11.7 9.3 %collective-permute-start.2 = (f32[65,4,1,128]{3,0,2,1:T(8,128)S(1)}, f32[65,4,1,128]{3,0,2,1:T(8,128)S(1)}, u32[]{:S(2)}, u32[]{:S(2)}) collective-permute-start(f32[65,4,1,128]{3,0,2,1:T(8,128)S(1)} %get-tuple-element.24), channel_id=1, source_target_pairs={{0,2},{2,4},{4,6},{1,3},{3,5},{5,7},{8,10},{10,12},{12,14},{9,11},... | collective-permute-start | bytes 399368 | tf_op jit(solution)/shard_map/ppermute | solution.py:17
  22.6 5.0 %copy-start.3 = (f32[64,2,8,128]{3,2,1,0:T(8,128)S(1)}, f32[64,2,8,128]{3,2,1,0:T(8,128)}, u32[]{:S(2)}) copy-start(f32[64,2,8,128]{3,2,1,0:T(8,128)} %param.14) | copy-start | bytes 1572868
  23.2 5.2 %collective-permute-start.4 = (f32[64,1,8,128]{3,0,2,1:T(8,128)S(1)}, f32[64,1,8,128]{3,0,2,1:T(8,128)S(1)}, u32[]{:S(2)}, u32[]{:S(2)}) collective-permute-start(f32[64,1,8,128]{3,0,2,1:T(8,128)S(1)} %get-tuple-element.35), channel_id=1, source_target_pairs={{8,0},{16,8},{24,16},{9,1},{17,9},{25,17},{10,2},{18,10},{26,18},{... | collective-permute-start | bytes 786440 | tf_op jit(solution)/shard_map/ppermute | solution.py:20
  24.5 4.3 %collective-permute-start.5 = (f32[64,1,8,128]{3,0,2,1:T(8,128)S(1)}, f32[64,1,8,128]{3,0,2,1:T(8,128)S(1)}, u32[]{:S(2)}, u32[]{:S(2)}) collective-permute-start(f32[64,1,8,128]{3,0,2,1:T(8,128)S(1)} %get-tuple-element.34), channel_id=1, source_target_pairs={{0,8},{8,16},{16,24},{1,9},{9,17},{17,25},{2,10},{10,18},{18,26},{... | collective-permute-start | bytes 786440 | tf_op jit(solution)/shard_map/ppermute | solution.py:17
  27.8 10.5 %copy-start = (f32[64,2,8,128]{3,0,2,1:T(8,128)}, f32[64,2,8,128]{3,0,2,1:T(8,128)S(1)}, u32[]{:S(2)}) copy-start(f32[64,2,8,128]{3,0,2,1:T(8,128)S(1)} %copy.95) | copy-start | bytes 1572868
  28.7 7.3 %collective-permute-start.6 = (f32[64,4,1,128]{3,0,2,1:T(8,128)S(1)}, f32[64,4,1,128]{3,0,2,1:T(8,128)S(1)}, u32[]{:S(2)}, u32[]{:S(2)}) collective-permute-start(f32[64,4,1,128]{3,0,2,1:T(8,128)S(1)} %get-tuple-element.29), channel_id=1, source_target_pairs={{2,0},{4,2},{6,4},{3,1},{5,3},{7,5},{10,8},{12,10},{14,12},{11,9},... | collective-permute-start | bytes 393224 | tf_op jit(solution)/shard_map/ppermute | solution.py:20
  30.0 7.5 %collective-permute-start.7 = (f32[64,4,1,128]{3,0,2,1:T(8,128)S(1)}, f32[64,4,1,128]{3,0,2,1:T(8,128)S(1)}, u32[]{:S(2)}, u32[]{:S(2)}) collective-permute-start(f32[64,4,1,128]{3,0,2,1:T(8,128)S(1)} %get-tuple-element.28), channel_id=1, source_target_pairs={{0,2},{2,4},{4,6},{1,3},{3,5},{5,7},{8,10},{10,12},{12,14},{9,11},... | collective-permute-start | bytes 393224 | tf_op jit(solution)/shard_map/ppermute | solution.py:17
  116.1 76.9 %copy-start.2 = (f32[64,2,8,128]{3,2,1,0:T(8,128)S(1)}, f32[64,2,8,128]{3,2,1,0:T(8,128)}, u32[]{:S(2)}) copy-start(f32[64,2,8,128]{3,2,1,0:T(8,128)} %param.13) | copy-start | bytes 1572868
  188.6 5.1 %collective-permute-start.8 = (f32[64,1,8,128]{3,0,2,1:T(8,128)S(1)}, f32[64,1,8,128]{3,0,2,1:T(8,128)S(1)}, u32[]{:S(2)}, u32[]{:S(2)}) collective-permute-start(f32[64,1,8,128]{3,0,2,1:T(8,128)S(1)} %get-tuple-element.33), channel_id=1, source_target_pairs={{8,0},{16,8},{24,16},{9,1},{17,9},{25,17},{10,2},{18,10},{26,18},{... | collective-permute-start | bytes 786440 | tf_op jit(solution)/shard_map/ppermute | solution.py:20
  189.9 4.2 %collective-permute-start.9 = (f32[64,1,8,128]{3,0,2,1:T(8,128)S(1)}, f32[64,1,8,128]{3,0,2,1:T(8,128)S(1)}, u32[]{:S(2)}, u32[]{:S(2)}) collective-permute-start(f32[64,1,8,128]{3,0,2,1:T(8,128)S(1)} %get-tuple-element.32), channel_id=1, source_target_pairs={{0,8},{8,16},{16,24},{1,9},{9,17},{17,25},{2,10},{10,18},{18,26},{... | collective-permute-start | bytes 786440 | tf_op jit(solution)/shard_map/ppermute | solution.py:17
  194.1 6.9 %collective-permute-start.10 = (f32[64,4,1,128]{3,0,2,1:T(8,128)S(1)}, f32[64,4,1,128]{3,0,2,1:T(8,128)S(1)}, u32[]{:S(2)}, u32[]{:S(2)}) collective-permute-start(f32[64,4,1,128]{3,0,2,1:T(8,128)S(1)} %get-tuple-element.27), channel_id=1, source_target_pairs={{2,0},{4,2},{6,4},{3,1},{5,3},{7,5},{10,8},{12,10},{14,12},{11,9},... | collective-permute-start | bytes 393224 | tf_op jit(solution)/shard_map/ppermute | solution.py:20
  195.4 7.1 %collective-permute-start.11 = (f32[64,4,1,128]{3,0,2,1:T(8,128)S(1)}, f32[64,4,1,128]{3,0,2,1:T(8,128)S(1)}, u32[]{:S(2)}, u32[]{:S(2)}) collective-permute-start(f32[64,4,1,128]{3,0,2,1:T(8,128)S(1)} %get-tuple-element.26), channel_id=1, source_target_pairs={{0,2},{2,4},{4,6},{1,3},{3,5},{5,7},{8,10},{10,12},{12,14},{9,11},... | collective-permute-start | bytes 393224 | tf_op jit(solution)/shard_map/ppermute | solution.py:17
  203.6 75.3 %slice-start = ((f32[64,2,8,128]{3,0,2,1:T(8,128)}), f32[64,1,8,128]{3,0,2,1:T(8,128)S(1)}, s32[]{:S(2)}) async-start(f32[64,2,8,128]{3,0,2,1:T(8,128)} %copy-done), calls=%async_computation | async-start | bytes 524288 | tf_op jit(solution)/shard_map/slice | solution.py:136
  203.6 77.5 %copy-start.1 = (f32[64,2,8,128]{3,0,2,1:T(8,128)S(1)}, f32[64,2,8,128]{3,0,2,1:T(8,128)}, u32[]{:S(2)}) copy-start(f32[64,2,8,128]{3,0,2,1:T(8,128)} %copy-done) | copy-start | bytes 1572868
  279.7 2.9 slice-start.1
  279.8 12.5 %collective-permute-start.12 = (f32[128,1,8,128]{3,0,2,1:T(8,128)}, f32[128,1,8,128]{3,0,2,1:T(8,128)S(1)}, u32[]{:S(2)}, u32[]{:S(2)}) collective-permute-start(f32[128,1,8,128]{3,0,2,1:T(8,128)} %pad_maximum_fusion.24), channel_id=1, source_target_pairs={{8,0},{16,8},{24,16},{9,1},{17,9},{25,17},{10,2},{18,10},{26,18},{... | collective-permute-start | bytes 1572872 | tf_op jit(solution)/shard_map/ppermute | solution.py:28
  282.6 8.1 %collective-permute-start.14 = (f32[128,2,1,128]{3,0,2,1:T(8,128)S(1)}, f32[128,2,1,128]{3,0,2,1:T(8,128)S(1)}, u32[]{:S(2)}, u32[]{:S(2)}) collective-permute-start(f32[128,2,1,128]{3,0,2,1:T(8,128)S(1)} %pad_maximum_fusion.36), channel_id=1, source_target_pairs={{2,0},{4,2},{6,4},{3,1},{5,3},{7,5},{10,8},{12,10},{14,12},{11,9},... | collective-permute-start | bytes 393224 | tf_op jit(solution)/shard_map/ppermute | solution.py:28
  290.8 7.1 %collective-permute-start.15 = (f32[2,128]{1,0:T(2,128)S(1)}, f32[2,128]{1,0:T(2,128)S(1)}, u32[]{:S(2)}, u32[]{:S(2)}) collective-permute-start(f32[2,128]{1,0:T(2,128)S(1)} %fusion.42), channel_id=1, source_target_pairs={{0,2},{2,4},{4,6},{1,3},{3,5},{5,7},{8,10},{10,12},{12,14},{9,11},... | collective-permute-start | bytes 3080 | tf_op jit(solution)/shard_map/ppermute | solution.py:28
  292.3 6.4 %collective-permute-start.13 = (f32[8,128]{1,0:T(8,128)S(1)}, f32[8,128]{1,0:T(8,128)S(1)}, u32[]{:S(2)}, u32[]{:S(2)}) collective-permute-start(f32[8,128]{1,0:T(8,128)S(1)} %fusion.40), channel_id=1, source_target_pairs={{0,8},{8,16},{16,24},{1,9},{9,17},{17,25},{2,10},{10,18},{18,26},{... | collective-permute-start | bytes 12296 | tf_op jit(solution)/shard_map/ppermute | solution.py:28
where the time goes:
time: 308 us; the launch traced here: 304 us
  blocking collectives  188 us (61%)
  other arithmetic  45.6 us (15%)
  starting transfers between devices  41.8 us (14%)
  waiting for transfers between devices  16 us (5%)
  matrix products  6.25 us (2%)
  local copies, waits for them, and re-layouts  5.23 us (2%)
    psum x1, blocking collectives, on_device(): res_gram = lax.psum(gram_of(residual, residual), ('gx', 'gy'))  63.8 us
    psum x1, blocking collectives, on_device(): curv_gram = lax.psum(gram_of(direction, image), ('gx', 'gy'))  61.2 us
    psum x1, blocking collectives, on_device(): new_gram = lax.psum(gram_of(residual, residual), ('gx', 'gy'))  58.1 us
    ppermute x6, starting transfers between devices, padded_2(): lax.ppermute(lax.slice_in_dim(block, block.shape[dim] - width, None, axis...  24.3 us
    another operation x9, other arithmetic, posdef_solve(): lower = jnp.linalg.cholesky(matrix)  19.6 us
    another operation x6, other arithmetic, posdef_solve(): lax.linalg.triangular_solve(lower, middle, left_side=True, lower=True, tr...  16.6 us
    ppermute x4, starting transfers between devices, shifted(): return lax.ppermute(x, axis, pairs)  9.74 us
    ppermute x6, starting transfers between devices, padded_2(): lax.ppermute(lax.slice_in_dim(block, 0, width, axis=dim), axis, backward)  7.75 us
  transfers between devices with their start and end apart: 16, of which 10 were waited for; matrix products, arithmetic and copies ran while one was open for 2% of the time, Pallas kernels for 0%

commit v1 on v0

v1 whole, which is shorter than its diff:
```python
import functools

import jax
import jax.numpy as jnp
from jax import lax
from jax.experimental import pallas as pl
from jax.experimental.pallas import tpu as pltpu
from jax.sharding import PartitionSpec as P

MESH = pl.DeviceIdType.MESH
INJECT = 4.0
F32 = jnp.float32
BF16 = jnp.bfloat16
HI = lax.Precision.HIGHEST


def split(x):
    hi = x.astype(BF16)
    return hi, (x - hi.astype(F32)).astype(BF16)


def nt(a, b):
    return lax.dot_general(a, b, (((1,), (1,)), ((), ())), preferred_element_type=F32)


def eliminate(lead, rest, off):
    row = lax.broadcasted_iota(jnp.int32, (8, 128), 0)
    count = len(lead)
    wide = len(rest) > 0

    def panel(_, carry):
        lead, rest = list(carry[0]), list(carry[1])
        cols = [
            [jnp.broadcast_to(tile[:, off + j : off + j + 1], (8, 128)) for tile in lead]
            for j in range(8)
        ]
        for j in range(8):
            col = cols[j]
            inv = 1.0 / jnp.broadcast_to(col[0][j : j + 1], (8, 128))

            def sweep(tiles):
                pivot = jnp.broadcast_to(tiles[0][j : j + 1], (8, 128)) * inv
                first = jnp.where(row == j, pivot, tiles[0] - col[0] * pivot)
                return [first] + [tiles[t] - col[t] * pivot for t in range(1, count)]

            for later in range(j + 1, 8):
                cols[later] = sweep(cols[later])
            lead = sweep(lead)
            if wide:
                rest = sweep(rest)
        lead = [pltpu.roll(tile, 120, 1) for tile in lead]
        lead = lead[1:] + lead[:1]
        if wide:
            rest = rest[1:] + rest[:1]
        return tuple(lead), tuple(rest)

    lead, rest = lax.fori_loop(0, count, panel, (tuple(lead), tuple(rest)))
    return jnp.concatenate(lead, axis=0), (jnp.concatenate(rest, axis=0) if wide else None)


def tiles_of(x):
    return [x[8 * t : 8 * t + 8] for t in range(x.shape[0] // 8)]


def kernel(
    sizes, x_in, adj_in, picked, x_out, grad_out,
    fx, fr, fq, fl, fs, cond, gbuf, r1, r2, gfin, gl, gr,
    send, recv, local, s1, v1, s2, v2, s3, v3, s4, v4,
):
    ngx, ngy, nsrc, cx, cy, cols = sizes
    gx, gy, src = lax.axis_index("gx"), lax.axis_index("gy"), lax.axis_index("src")

    def peer(axis, index):
        return {"gx": (index, gy, src), "gy": (gx, index, src), "src": (gx, gy, index)}[axis]

    barrier = pltpu.get_barrier_semaphore()
    groups = (("gx", gx, ngx), ("gy", gy, ngy), ("src", src, nsrc))
    for axis, me, count in groups:
        for k in range(1, count):
            pl.semaphore_signal(
                barrier, inc=1, device_id=peer(axis, lax.rem(me + k, count)), device_id_type=MESH
            )
    pl.semaphore_wait(barrier, ngx + ngy + nsrc - 3)

    low_x = (0, slice(1, cy + 1))
    inner = (slice(1, cx + 1), slice(1, cy + 1))

    def exchange(step, ref, buf, base):
        ys = pl.ds(base, cy)
        xs = pl.ds(base, cx)
        hy, hx = pl.ds(1, cy), pl.ds(1, cx)
        moves = (
            (gx > 0, gx < ngx - 1, ref.at[base, ys], buf.at[cx + 1, hy], ("gx", gx - 1)),
            (gx < ngx - 1, gx > 0, ref.at[base + cx - 1, ys], buf.at[0, hy], ("gx", gx + 1)),
            (gy > 0, gy < ngy - 1, ref.at[xs, base], buf.at[hx, cy + 1], ("gy", gy - 1)),
            (gy < ngy - 1, gy > 0, ref.at[xs, base + cy - 1], buf.at[hx, 0], ("gy", gy + 1)),
        )
        made = []
        for n, (sends, gets, source, target, (axis, index)) in enumerate(moves):
            limit = ngx if axis == "gx" else ngy
            index = jnp.clip(index, 0, limit - 1)
            copy = pltpu.make_async_remote_copy(
                src_ref=source, dst_ref=target, send_sem=send.at[step, n],
                recv_sem=recv.at[step, n], device_id=peer(axis, index), device_id_type=MESH,
            )
            made.append((sends, gets, copy, target))

            @pl.when(sends)
            def _():
                copy.start()

        def arrive():
            for sends, gets, copy, target in made:
                @pl.when(gets)
                def _():
                    copy.wait_recv()

                @pl.when(jnp.logical_not(gets))
                def _():
                    target[...] = jnp.zeros(target.shape, F32)

        def leave():
            for sends, gets, copy, target in made:
                @pl.when(sends)
                def _():
                    copy.wait_send()

        return arrive, leave

    arrive0, leave0 = exchange(0, x_in, fx, 0)
    load_x = pltpu.make_async_copy(x_in, fx.at[pl.ds(1, cx), pl.ds(1, cy)], local.at[0])
    load_x.start()
    load_l = pltpu.make_async_copy(adj_in, fl.at[pl.ds(1, cx), pl.ds(1, cy)], local.at[1])
    load_l.start()
    load_x.wait()
    arrive0()

    lane = lax.broadcasted_iota(jnp.int32, (8, 128), 1)

    def each_cell(body):
        def step(i, carry):
            body(i // cy, lax.rem(i, cy))
            return carry

        lax.fori_loop(0, cx * cy, step, 0)

    def conductance(x, y):
        def sig(i, j):
            return fx[i, j, cols:, :]

        mid = sig(x + 1, y + 1)
        parts = [
            0.5 * (mid + sig(x, y + 1)),
            0.5 * (mid + sig(x + 2, y + 1)),
            0.5 * (mid + sig(x + 1, y)),
            0.5 * (mid + sig(x + 1, y + 2)),
            0.5 * (mid + jnp.where(lane == 0, 0.0, pltpu.roll(mid, 1, 1))),
            0.5 * (mid + jnp.where(lane == 127, 0.0, pltpu.roll(mid, 127, 1))),
        ]
        total = parts[0] + parts[1] + (parts[2] + parts[3]) + (parts[4] + parts[5])
        parts[4] = jnp.where(lane == 0, 0.0, parts[4])
        parts[5] = jnp.where(lane == 127, 0.0, parts[5])
        for n, part in enumerate(parts + [total]):
            cond[x, y, n] = part

    def image(buf, x, y):
        def at(i, j):
            return buf[i, j, :cols, :].reshape(cols // 8, 8, 128)

        mid = at(x + 1, y + 1)
        flat = mid.reshape(cols, 128)
        down = pltpu.roll(flat, 1, 1).reshape(cols // 8, 8, 128)
        up = pltpu.roll(flat, 127, 1).reshape(cols // 8, 8, 128)
        c = [cond[x, y, n][None] for n in range(7)]
        out = c[6] * mid - (
            c[0] * at(x, y + 1) + c[1] * at(x + 2, y + 1)
            + (c[2] * at(x + 1, y) + c[3] * at(x + 1, y + 2))
            + (c[4] * down + c[5] * up)
        )
        return out.reshape(cols, 128)

    each_cell(conductance)

    lane_c = lax.broadcasted_iota(jnp.int32, (cols, 128), 1)

    def residual(x, y):
        base = ((gx * cx + x) * (ngy * cy) + gy * cy + y) * 128
        right = jnp.where(picked[0] - base == lane_c, INJECT, 0.0) - jnp.where(
            picked[1] - base == lane_c, INJECT, 0.0
        )
        fr[x + 1, y + 1] = right - image(fx, x, y)

    each_cell(residual)
    arrive1, leave1 = exchange(1, fr, fr, 1)
    arrive1()

    def first(x, y):
        fq[x + 1, y + 1] = image(fr, x, y)

    each_cell(first)
    arrive2, leave2 = exchange(2, fq, fq, 1)
    load_l.wait()
    arrive3, leave3 = exchange(3, fl, fl, 1)
    arrive2()

    def second(x, y):
        fs[x, y] = image(fq, x, y)

    each_cell(second)

    def gram(i, carry):
        x, y = i // (cy // 2), 2 * lax.rem(i, cy // 2)

        def pair(buf, o):
            return split(jnp.concatenate([buf[x + o, y + o], buf[x + o, y + o + 1]], axis=1))

        (rh, rl), (qh, ql), (sh, sl) = pair(fr, 1), pair(fq, 1), pair(fs, 0)
        rqh, rql = jnp.concatenate([rh, qh], axis=0), jnp.concatenate([rl, ql], axis=0)
        qsh, qsl = jnp.concatenate([qh, sh], axis=0), jnp.concatenate([ql, sl], axis=0)
        a = nt(rh, rqh) + (nt(rh, rql) + nt(rl, rqh))
        b = nt(qh, qsh) + (nt(qh, qsl) + nt(ql, qsh))
        return carry[0] + a, carry[1] + b

    zero = jnp.zeros((cols, 2 * cols), F32)
    ga, gb = lax.fori_loop(0, cx * cy // 2, gram, (zero, zero))
    rows = 2 * cols // ngx
    both = jnp.concatenate([ga, gb], axis=0)
    gbuf[...] = both.reshape(ngx, rows, 2 * cols)

    made = []
    for k in range(1, ngx):
        to = lax.rem(gx + k, ngx)
        copy = pltpu.make_async_remote_copy(
            src_ref=gbuf.at[to], dst_ref=r1.at[k - 1], send_sem=s1.at[k - 1],
            recv_sem=v1.at[k - 1], device_id=peer("gx", to), device_id_type=MESH,
        )
        copy.start()
        made.append(copy)
    share = gbuf[gx]
    for k, copy in enumerate(made):
        copy.wait_recv()
        share = share + r1[k]
    r2[gy] = share
    late = list(made)
    made = []
    for k in range(1, ngy):
        to = lax.rem(gy + k, ngy)
        copy = pltpu.make_async_remote_copy(
            src_ref=r2.at[gy], dst_ref=r2.at[gy], send_sem=s2.at[k - 1],
            recv_sem=v2.at[k - 1], device_id=peer("gy", to), device_id_type=MESH,
        )
        copy.start()
        made.append(copy)
    late += made
    for copy in made:
        copy.wait_recv()
    total = r2[0]
    for k in range(1, ngy):
        total = total + r2[k]
    gfin[gx] = total
    made = []
    for k in range(1, ngx):
        to = lax.rem(gx + k, ngx)
        copy = pltpu.make_async_remote_copy(
            src_ref=gfin.at[gx], dst_ref=gfin.at[gx], send_sem=s3.at[k - 1],
            recv_sem=v3.at[k - 1], device_id=peer("gx", to), device_id_type=MESH,
        )
        copy.start()
        made.append(copy)
    late += made
    for copy in made:
        copy.wait_recv()

    whole = gfin[...].reshape(2 * cols, 2 * cols)
    top, low = whole[:cols], whole[cols:]
    lead, rest = eliminate(tiles_of(top), tiles_of(low), cols)
    alpha = lead[:, cols:]
    inv2 = rest[:, :cols]
    g2, g3, g1 = low[:, :cols], low[:, cols:], top[:, cols:]
    prod = jnp.dot(
        g2, jnp.concatenate([alpha, inv2], axis=1), precision=HI, preferred_element_type=F32
    )
    system = jnp.concatenate([g1, g3], axis=1) - prod
    lead, _ = eliminate(tiles_of(system), [], cols)
    c1 = lead[:, cols:]
    c0 = alpha - jnp.dot(inv2, c1, precision=HI, preferred_element_type=F32)
    stacked = jnp.concatenate([c0, c1], axis=0)
    stacked = jnp.concatenate([stacked, jnp.zeros_like(stacked)], axis=1).T[:cols]
    ch, cl = split(stacked)
    factors = jnp.concatenate(
        [
            jnp.concatenate([ch, ch], axis=1),
            jnp.concatenate([cl, jnp.zeros_like(cl)], axis=1),
        ],
        axis=0,
    )

    def advance(x, y):
        def pair(buf):
            return jnp.concatenate([buf[x, y], buf[x, y + 1]], axis=1)

        hi, lo = split(jnp.concatenate([pair(fr), pair(fq)], axis=0))
        out = jnp.dot(factors, jnp.concatenate([hi, lo], axis=0), preferred_element_type=F32)
        out = out[:cols] + out[cols:]
        fx[x, y, :cols, :] = fx[x, y, :cols, :] + out[:, :128]
        fx[x, y + 1, :cols, :] = fx[x, y + 1, :cols, :] + out[:, 128:]

    def inner_rows(i, carry):
        for x in range(1, cx + 1):
            advance(x, 2 * i)
        return carry

    def outer_rows(i, carry):
        for x in (0, cx + 1):
            advance(x, 2 * i + 1)
        return carry

    lax.fori_loop(0, (cy + 2) // 2, inner_rows, 0)
    store = pltpu.make_async_copy(
        fx.at[pl.ds(1, cx), pl.ds(1, cy), pl.ds(0, cols)], x_out, local.at[2]
    )
    store.start()
    lax.fori_loop(0, cy // 2, outer_rows, 0)

    arrive3()

    def field(i, ys):
        return fx[i, ys, :cols, :], fl[i, ys, :, :]

    mid_y = slice(1, cy + 1)
    term_x = []
    for i in range(cx + 1):
        (u0, l0), (u1, l1) = field(i, mid_y), field(i + 1, mid_y)
        term_x.append(jnp.sum((u1 - u0) * (l1 - l0), axis=1))
    lane_y = lax.broadcasted_iota(jnp.int32, (cy, 128), 1)
    for i in range(cx):
        (u0, l0), (u1, l1) = field(i + 1, slice(0, cy + 1)), field(i + 1, slice(1, cy + 2))
        term_y = jnp.sum((u1 - u0) * (l1 - l0), axis=1)
        u, l = field(i + 1, mid_y)
        u, l = u.reshape(cy * cols, 128), l.reshape(cy * cols, 128)
        lane_f = lax.broadcasted_iota(jnp.int32, u.shape, 1)
        du = u - jnp.where(lane_f == 0, 0.0, pltpu.roll(u, 1, 1))
        dl = l - jnp.where(lane_f == 0, 0.0, pltpu.roll(l, 1, 1))
        term_z = jnp.sum((du * dl).reshape(cy, cols, 128), axis=1)
        last = jnp.sum((u * l).reshape(cy, cols, 128), axis=1)
        upper = jnp.where(lane_y == 127, last, pltpu.roll(term_z, 127, 1))
        gl[i] = (-0.5 / cols) * (
            term_x[i] + term_x[i + 1] + term_y[:-1] + term_y[1:] + term_z + upper
        )

    made = []
    for k in range(1, nsrc):
        copy = pltpu.make_async_remote_copy(
            src_ref=gl, dst_ref=gr.at[k - 1], send_sem=s4.at[k - 1], recv_sem=v4.at[k - 1],
            device_id=peer("src", lax.rem(src + k, nsrc)), device_id_type=MESH,
        )
        copy.start()
        made.append(copy)
    late += made
    summed = gl[...]
    for k, copy in enumerate(made):
        copy.wait_recv()
        summed = summed + gr[k]
    width = 128 // nsrc
    part = summed[:, :, :width]
    for k in range(1, nsrc):
        part = jnp.where(src == k, summed[:, :, k * width : (k + 1) * width], part)
    grad_out[...] = part
    store.wait()
    leave0()
    leave1()
    leave2()
    leave3()
    for copy in late:
        copy.wait_send()


def on_device(sizes, conductivity, electrodes, pair_order, initial_fields, adjoint_fields):
    ngx, ngy, nsrc = sizes
    cols, cx, cy, cz = initial_fields.shape
    pairs = jnp.arange(electrodes.shape[0], dtype=jnp.int32)
    hit = pair_order[:, None] == pairs[None, :]
    picked = jnp.sum(jnp.where(hit[None], electrodes.T[:, None, :], 0), axis=-1)
    picked = jnp.broadcast_to(picked[:, :, None], (2, cols, cz))
    x_in = jnp.concatenate(
        [
            initial_fields.transpose(1, 2, 0, 3),
            jnp.broadcast_to(conductivity[:, :, None, :], (cx, cy, 8, cz)),
        ],
        axis=2,
    )
    adj_in = adjoint_fields.transpose(1, 2, 0, 3)
    rows = 2 * cols // ngx
    dma = pltpu.SemaphoreType.DMA
    full = (cx + 2, cy + 2, cols, cz)
    x_out, grad = pl.pallas_call(
        functools.partial(kernel, (ngx, ngy, nsrc, cx, cy, cols)),
        out_shape=(
            jax.ShapeDtypeStruct((cx, cy, cols, cz), F32),
            jax.ShapeDtypeStruct((cx, cy, cz // nsrc), F32),
        ),
        in_specs=[
            pl.BlockSpec(memory_space=pl.ANY),
            pl.BlockSpec(memory_space=pl.ANY),
            pl.BlockSpec(memory_space=pltpu.VMEM),
        ],
        out_specs=(
            pl.BlockSpec(memory_space=pl.ANY),
            pl.BlockSpec(memory_space=pltpu.VMEM),
        ),
        scratch_shapes=[
            pltpu.VMEM((cx + 2, cy + 2, cols + 8, cz), F32),
            pltpu.VMEM(full, F32),
            pltpu.VMEM(full, F32),
            pltpu.VMEM(full, F32),
            pltpu.VMEM((cx, cy, cols, cz), F32),
            pltpu.VMEM((cx, cy, 7, 8, cz), F32),
            pltpu.VMEM((ngx, rows, 2 * cols), F32),
            pltpu.VMEM((ngx - 1, rows, 2 * cols), F32),
            pltpu.VMEM((ngy, rows, 2 * cols), F32),
            pltpu.VMEM((ngx, rows, 2 * cols), F32),
            pltpu.VMEM((cx, cy, cz), F32),
            pltpu.VMEM((nsrc - 1, cx, cy, cz), F32),
            dma((4, 4)), dma((4, 4)), dma((3,)),
            dma((ngx - 1,)), dma((ngx - 1,)),
            dma((ngy - 1,)), dma((ngy - 1,)),
            dma((ngx - 1,)), dma((ngx - 1,)),
            dma((nsrc - 1,)), dma((nsrc - 1,)),
        ],
        compiler_params=pltpu.CompilerParams(
            collective_id=0, has_side_effects=True, vmem_limit_bytes=32 * 1024 * 1024
        ),
        cost_estimate=pl.CostEstimate(
            flops=4 * 10**8, bytes_accessed=2 * 10**6, transcendentals=0
        ),
    )(x_in, adj_in, picked)
    return x_out.transpose(2, 0, 1, 3), grad


def solution(mesh):
    sizes = (mesh.shape["gx"], mesh.shape["gy"], mesh.shape["src"])
    field = P("src", "gx", "gy", None)
    return jax.shard_map(
        functools.partial(on_device, sizes),
        mesh=mesh,
        in_specs=(P("gx", "gy", None), P(), P("src"), field, field),
        out_specs=(field, P("gx", "gy", "src")),
        check_vma=False,
    )
```

time: 308 us -> 55 us (0.18); the launches traced: 304 us -> 54.7 us
  blocking collectives: 188 us -> 0 us
  Pallas kernels: 0 us -> 47.8 us
  other arithmetic: 45.6 us -> 0.22 us
  starting transfers between devices: 41.8 us -> 0 us
  waiting for transfers between devices: 16 us -> 0 us
  matrix products: 6.25 us -> 0 us
    psum x4 -> x0, blocking collectives: 188 us -> none  [the longest x1 63.8 us: on_device(): res_gram = lax.psum(gram_of(residual, residual), ('gx', 'gy'))]
    pallas_call x0 -> x1, Pallas kernels: none -> 47.8 us  [on_device(): pl.pallas_call(functools.partial(kernel, (ngx, ngy, nsrc, cx, cy, cols)),...]
    ppermute x16 -> x0, starting transfers between devices: 41.8 us -> none  [the longest x6 24.3 us: padded_2(): lax.ppermute(lax.slice_in_dim(block, block.shape[dim] - width, None, axis...]
    another operation x18 -> x0, other arithmetic: 36.4 us -> none  [the longest x9 19.6 us: posdef_solve(): lower = jnp.linalg.cholesky(matrix)]
    ppermute x16 -> x0, waiting for transfers between devices: 16 us -> none  [the longest x4 6.68 us: shifted(): return lax.ppermute(x, axis, pairs)]
    dot_general x8 -> x0, matrix products: 4.8 us -> none  [the longest x4 2.41 us: gram_of(): jnp.einsum('axyz,bxyz->ab', left, right, precision=lax.Precision.HIGHEST)]
    concatenate x8 -> x1, other arithmetic: 3.92 us -> 0.04 us  [on_device(): jnp.concatenate([initial_fields.transpose(1, 2, 0, 3), jnp.broadcast_to(c...]
  transfers between devices with their start and end apart: 16 -> 0, of which waited for: 10 -> 0; matrix products, arithmetic and copies ran while one was open for 2% -> 0% of each run, Pallas kernels for 0% -> 0%
where the time goes in v1:
time: 55 us; the launch traced here: 54.7 us
  Pallas kernels  47.8 us (87%)
  local copies, waits for them, and re-layouts  6.02 us (11%)
  between operations  0.68 us (1%)
    pallas_call x1, Pallas kernels, on_device(): pl.pallas_call(functools.partial(kernel, (ngx, ngy, nsrc, cx, cy, cols)),...  47.8 us
    unnamed x12, local copies, waits for them, and re-layouts  5.94 us

profile of v1, /device:TPU:0, one launch (start us, length us, event | category | flops | bytes accessed | tf_op | source)
XLA Modules:
  0.0 54.7 jit_solution(9035211156294786569)
XLA Ops:
  0.6 0.0 copy-start.3
  0.6 0.6 %copy-done.3 = s32[64]{0:T(128)S(1)} copy-done((s32[64]{0:T(128)S(1)}, s32[64]{0:T(128)}, u32[]{:S(2)}) %copy-start.3) | copy-done | bytes 280
  1.3 0.0 copy-start.2
  1.3 0.1 iota_compare_fusion
  1.4 0.6 %copy-done.2 = s32[128,2]{0,1:T(2,128)S(1)} copy-done((s32[128,2]{0,1:T(2,128)S(1)}, s32[128,2]{0,1:T(2,128)}, u32[]{:S(2)}) %copy-start.2) | copy-done | bytes 1048
  2.0 0.1 select_reduce_fusion
  2.1 0.0 copy-start.1
  2.1 0.1 broadcast_in_dim.40.picked
  2.2 0.6 %copy-done.1 = f32[2,8,128]{2,1,0:T(8,128)S(1)} copy-done((f32[2,8,128]{2,1,0:T(8,128)S(1)}, f32[2,8,128]{2,1,0:T(8,128)}, u32[]{:S(2)}) %copy-start.1) | copy-done | bytes 8216
  2.8 1.2 %copy.16 = f32[64,2,8,128]{3,0,2,1:T(8,128)S(1)} copy(f32[64,2,8,128]{3,2,1,0:T(8,128)} %param.8) | data formatting | bytes 1048576 | tf_op args[3]
  4.0 0.0 copy-start
  4.1 1.0 %copy-done = f32[64,2,8,128]{3,2,1,0:T(8,128)S(1)} copy-done((f32[64,2,8,128]{3,2,1,0:T(8,128)S(1)}, f32[64,2,8,128]{3,2,1,0:T(8,128)}, u32[]{:S(2)}) %copy-start) | copy-done | bytes 524312
  5.0 0.2 copy.15
  5.2 47.8 %shard_map.68 = (f32[2,8,64,128]{3,2,1,0:T(8,128)S(1)}, f32[2,8,64]{2,1,0:T(8,128)S(1)}) custom-call(f32[2,8,72,128]{3,2,1,0:T(8,128)S(1)} %pad_maximum_fusion.x_in, f32[2,8,64,128]{3,2,1,0:T(8,128)S(1)} %bitcast.9, s32[2,64,128]{2,1,0:T(8,128)S(1)} %broadcast_in_dim.40.picked), custom_call_target="tpu_custom_call" | custom-call | flops 400000000 | bytes 2000000 | tf_op jit(solution)/shard_map/pallas_call | solution.py:396
  53.0 1.1 %copy.12 = f32[64,2,8,128]{3,2,1,0:T(8,128)} copy(f32[64,2,8,128]{3,0,2,1:T(8,128)S(1)} %bitcast.8) | data formatting | bytes 1048576
  54.1 0.6 %copy.18 = f32[2,8,64]{2,1,0:T(8,128)} copy(f32[2,8,64]{2,1,0:T(8,128)S(1)} %get-tuple-element.13) | data formatting | bytes 8192
  (2 shorter events, 0.0 us)
Async XLA Ops:
  0.6 0.7 %copy-start.3 = (s32[64]{0:T(128)S(1)}, s32[64]{0:T(128)}, u32[]{:S(2)}) copy-start(s32[64]{0:T(128)} %param.7) | copy-start | bytes 772
  1.3 0.7 %copy-start.2 = (s32[128,2]{0,1:T(2,128)S(1)}, s32[128,2]{0,1:T(2,128)}, u32[]{:S(2)}) copy-start(s32[128,2]{0,1:T(2,128)} %param.6) | copy-start | bytes 3076
  2.1 0.7 %copy-start.1 = (f32[2,8,128]{2,1,0:T(8,128)S(1)}, f32[2,8,128]{2,1,0:T(8,128)}, u32[]{:S(2)}) copy-start(f32[2,8,128]{2,1,0:T(8,128)} %param.5) | copy-start | bytes 24580
  4.0 1.0 %copy-start = (f32[64,2,8,128]{3,2,1,0:T(8,128)S(1)}, f32[64,2,8,128]{3,2,1,0:T(8,128)}, u32[]{:S(2)}) copy-start(f32[64,2,8,128]{3,2,1,0:T(8,128)} %param.9) | copy-start | bytes 1572868

commit v2 on v1

v2 whole, which is shorter than its diff:
```python
import functools

import jax
import jax.numpy as jnp
from jax import lax
from jax.experimental import pallas as pl
from jax.experimental.pallas import tpu as pltpu
from jax.sharding import PartitionSpec as P

MESH = pl.DeviceIdType.MESH
INJECT = 4.0
F32 = jnp.float32
BF16 = jnp.bfloat16
HI = lax.Precision.HIGHEST


def split(x):
    hi = x.astype(BF16)
    return hi, (x - hi.astype(F32)).astype(BF16)


def nt(a, b):
    return lax.dot_general(a, b, (((1,), (1,)), ((), ())), preferred_element_type=F32)


def eliminate(lead, rest, off, panels):
    row = lax.broadcasted_iota(jnp.int32, (8, 128), 0)
    count = len(lead)
    wide = len(rest) > 0

    def spread(tile, j):
        return jnp.broadcast_to(tile[j : j + 1], (8, 128))

    def panel(_, carry):
        lead, rest = list(carry[0]), list(carry[1])
        cols = [
            [jnp.broadcast_to(tile[:, off + j : off + j + 1], (8, 128)) for tile in lead]
            for j in range(8)
        ]
        for j in range(0, 8, 2):
            a, b = cols[j], cols[j + 1]
            a0, a1, b0, b1 = spread(a[0], j), spread(a[0], j + 1), spread(b[0], j), spread(b[0], j + 1)
            inv = 1.0 / (a0 * b1 - a1 * b0)
            i00, i01, i10, i11 = b1 * inv, b0 * inv, a1 * inv, a0 * inv

            def sweep(tiles):
                r0, r1 = spread(tiles[0], j), spread(tiles[0], j + 1)
                n0 = i00 * r0 - i01 * r1
                n1 = i11 * r1 - i10 * r0
                out = [tiles[t] - (a[t] * n0 + b[t] * n1) for t in range(count)]
                out[0] = jnp.where(row == j, n0, jnp.where(row == j + 1, n1, out[0]))
                return out

            for later in range(j + 2, 8):
                cols[later] = sweep(cols[later])
            lead = sweep(lead)
            if wide:
                rest = sweep(rest)
        lead = [pltpu.roll(tile, 120, 1) for tile in lead]
        lead = lead[1:] + lead[:1]
        if wide:
            rest = rest[1:] + rest[:1]
        return tuple(lead), tuple(rest)

    return lax.fori_loop(0, panels, panel, (tuple(lead), tuple(rest)))


def tiles_of(x):
    return [x[8 * t : 8 * t + 8] for t in range(x.shape[0] // 8)]


PARTS = 2


def kernel(
    sizes, sig_in, elec_in, order_in, x_in, adj_in, x_out, grad_out,
    fx, fr, fq, fl, fs, cond, sig, elec, order, picked,
    gbufs, r1s, r2s, gfins, gl, gr,
    send, recv, local, s1s, v1s, s2s, v2s, s3s, v3s, s4, v4,
):
    ngx, ngy, nsrc, cx, cy, cols = sizes
    gx, gy, src = lax.axis_index("gx"), lax.axis_index("gy"), lax.axis_index("src")
    half = cols // PARTS

    def peer(axis, index):
        return {"gx": (index, gy, src), "gy": (gx, index, src), "src": (gx, gy, index)}[axis]

    small = [
        pltpu.make_async_copy(sig_in, sig, local.at[0]),
        pltpu.make_async_copy(elec_in, elec, local.at[1]),
        pltpu.make_async_copy(order_in, order, local.at[2]),
    ]
    for copy in small:
        copy.start()

    def load(source, buf, low, count, sem):
        for x in range(cx):
            for y in range(cy):
                pltpu.make_async_copy(
                    source.at[pl.ds(low, count), x, y],
                    buf.at[x + 1, y + 1, pl.ds(low, count)],
                    sem,
                ).start()
        whole = buf.at[pl.ds(1, cx), pl.ds(1, cy), pl.ds(low, count)]
        return pltpu.make_async_copy(whole, whole, sem)

    loads = [load(x_in, fx, h * half, half, local.at[3 + h]) for h in range(PARTS)]

    barrier = pltpu.get_barrier_semaphore()
    groups = (("gx", gx, ngx), ("gy", gy, ngy), ("src", src, nsrc))
    for axis, me, count in groups:
        for k in range(1, count):
            pl.semaphore_signal(
                barrier, inc=1, device_id=peer(axis, lax.rem(me + k, count)), device_id_type=MESH
            )

    def exchange(step, buf, low, count):
        zs = pl.ds(low, count)
        hx, hy = pl.ds(1, cx), pl.ds(1, cy)
        moves = (
            (gx > 0, gx < ngx - 1, buf.at[1, hy, zs], buf.at[cx + 1, hy, zs], ("gx", gx - 1)),
            (gx < ngx - 1, gx > 0, buf.at[cx, hy, zs], buf.at[0, hy, zs], ("gx", gx + 1)),
            (gy > 0, gy < ngy - 1, buf.at[hx, 1, zs], buf.at[hx, cy + 1, zs], ("gy", gy - 1)),
            (gy < ngy - 1, gy > 0, buf.at[hx, cy, zs], buf.at[hx, 0, zs], ("gy", gy + 1)),
        )
        made = []
        for n, (sends, gets, source, target, (axis, index)) in enumerate(moves):
            limit = ngx if axis == "gx" else ngy
            index = jnp.clip(index, 0, limit - 1)
            copy = pltpu.make_async_remote_copy(
                src_ref=source, dst_ref=target, send_sem=send.at[step, n],
                recv_sem=recv.at[step, n], device_id=peer(axis, index), device_id_type=MESH,
            )
            made.append((sends, gets, copy, target))

            @pl.when(sends)
            def _():
                copy.start()

            @pl.when(jnp.logical_not(gets))
            def _():
                target[...] = jnp.zeros(target.shape, F32)

        def arrive():
            for sends, gets, copy, target in made:
                @pl.when(gets)
                def _():
                    copy.wait_recv()

        def leave():
            for sends, gets, copy, target in made:
                @pl.when(sends)
                def _():
                    copy.wait_send()

        leaves.append(leave)
        return arrive

    leaves = []
    for copy in small:
        copy.wait()
    for x in range(cx):
        for y in range(cy):
            fx[x + 1, y + 1, cols:, :] = jnp.broadcast_to(sig[x, y : y + 1, :], (8, 128))
    pl.semaphore_wait(barrier, ngx + ngy + nsrc - 3)
    arrive_sig = exchange(0, fx, cols, 8)
    arrive_x = []
    for h in range(PARTS):
        loads[h].wait()
        arrive_x.append(exchange(1 + h, fx, h * half, half))
    load_l = load(adj_in, fl, 0, cols, local.at[3 + PARTS])

    lane = lax.broadcasted_iota(jnp.int32, (8, 128), 1)

    pairs = elec.shape[1]
    slot = jnp.concatenate([order[...], jnp.full((1, 128 - cols), -1, jnp.int32)], axis=1)
    hit = lax.broadcasted_iota(jnp.int32, (pairs, 128), 0) == jnp.broadcast_to(slot, (pairs, 128))
    table = jnp.concatenate([elec[...].astype(F32), jnp.zeros((6, pairs), F32)], axis=0)
    cells = jnp.dot(table, hit.astype(F32), precision=HI, preferred_element_type=F32).T
    for n in range(2):
        picked[n] = jnp.broadcast_to(cells[:cols, n : n + 1], (cols, 128)).astype(jnp.int32)

    group = 4

    def each_cell(body):
        def step(i, carry):
            x, y = i // (cy // group), group * lax.rem(i, cy // group)
            for k in range(group):
                body(x, y + k)
            return carry

        lax.fori_loop(0, cx * cy // group, step, 0)

    def conductance(x, y):
        def sig_at(i, j):
            return fx[i, j, cols:, :]

        mid = sig_at(x + 1, y + 1)
        parts = [
            0.5 * (mid + sig_at(x, y + 1)),
            0.5 * (mid + sig_at(x + 2, y + 1)),
            0.5 * (mid + sig_at(x + 1, y)),
            0.5 * (mid + sig_at(x + 1, y + 2)),
            0.5 * (mid + jnp.where(lane == 0, 0.0, pltpu.roll(mid, 1, 1))),
            0.5 * (mid + jnp.where(lane == 127, 0.0, pltpu.roll(mid, 127, 1))),
        ]
        total = parts[0] + parts[1] + (parts[2] + parts[3]) + (parts[4] + parts[5])
        parts[4] = jnp.where(lane == 0, 0.0, parts[4])
        parts[5] = jnp.where(lane == 127, 0.0, parts[5])
        for n, part in enumerate(parts + [total]):
            cond[x, y, n] = part

    def image(buf, x, y, h):
        rows = slice(h * half, (h + 1) * half)

        def at(i, j):
            return buf[i, j, rows, :].reshape(half // 8, 8, 128)

        flat = buf[x + 1, y + 1, rows, :]
        mid = flat.reshape(half // 8, 8, 128)
        down = pltpu.roll(flat, 1, 1).reshape(half // 8, 8, 128)
        up = pltpu.roll(flat, 127, 1).reshape(half // 8, 8, 128)
        c = [cond[x, y, n][None] for n in range(7)]
        out = c[6] * mid - (
            c[0] * at(x, y + 1) + c[1] * at(x + 2, y + 1)
            + (c[2] * at(x + 1, y) + c[3] * at(x + 1, y + 2))
            + (c[4] * down + c[5] * up)
        )
        return out.reshape(half, 128)

    arrive_sig()
    each_cell(conductance)

    lane_c = lax.broadcasted_iota(jnp.int32, (half, 128), 1)

    arrive_r = []
    for h in range(PARTS):
        rows = slice(h * half, (h + 1) * half)

        def residual(x, y):
            base = ((gx * cx + x) * (ngy * cy) + gy * cy + y) * 128
            right = jnp.where(picked[0, rows] - base == lane_c, INJECT, 0.0) - jnp.where(
                picked[1, rows] - base == lane_c, INJECT, 0.0
            )
            fr[x + 1, y + 1, rows, :] = right - image(fx, x, y, h)

        arrive_x[h]()
        each_cell(residual)
        arrive_r.append(exchange(1 + PARTS + h, fr, h * half, half))

    arrive_q = []
    for h in range(PARTS):
        def first(x, y):
            fq[x + 1, y + 1, slice(h * half, (h + 1) * half), :] = image(fr, x, y, h)

        arrive_r[h]()
        each_cell(first)
        arrive_q.append(exchange(1 + 2 * PARTS + h, fq, h * half, half))

    load_l.wait()
    arrive_l = exchange(1 + 3 * PARTS, fl, 0, cols)

    def wide_of(buf, o, i):
        x, y = i // (cy // group), group * lax.rem(i, cy // group)
        return split(
            jnp.concatenate([buf[x + o, y + o + k] for k in range(group)], axis=1)
        )

    def times(left, right):
        return nt(left[0], right[0]) + (nt(left[0], right[1]) + nt(left[1], right[0]))

    def early(i, carry):
        r, q = wide_of(fr, 1, i), wide_of(fq, 1, i)
        rq = [jnp.concatenate([u, v], axis=0) for u, v in zip(r, q)]
        return carry[0] + times(r, rq), carry[1] + times(q, q)

    steps = cx * cy // group
    square, double = jnp.zeros((cols, cols), F32), jnp.zeros((cols, 2 * cols), F32)
    g01, g22 = lax.fori_loop(0, steps, early, (double, square))

    late = []

    def reduction(n, value):
        gbuf, r1, r2, gfin = gbufs[n], r1s[n], r2s[n], gfins[n]
        s1, v1, s2, v2, s3, v3 = s1s.at[n], v1s.at[n], s2s.at[n], v2s.at[n], s3s.at[n], v3s.at[n]
        gbuf[...] = value.reshape(gbuf.shape)

        def spread(axis, me, count, pieces, sems, waits):
            made = []
            for k in range(1, count):
                to = lax.rem(me + k, count)
                source, target = pieces(k, to)
                copy = pltpu.make_async_remote_copy(
                    src_ref=source, dst_ref=target, send_sem=sems.at[k - 1],
                    recv_sem=waits.at[k - 1], device_id=peer(axis, to), device_id_type=MESH,
                )
                copy.start()
                made.append(copy)
            late.extend(made)
            return made

        made = spread("gx", gx, ngx, lambda k, to: (gbuf.at[to], r1.at[k - 1]), s1, v1)

        def second():
            share = gbuf[gx]
            for k, copy in enumerate(made):
                copy.wait_recv()
                share = share + r1[k]
            r2[gy] = share
            made[:] = spread("gy", gy, ngy, lambda k, to: (r2.at[gy], r2.at[gy]), s2, v2)

        def third():
            for copy in made:
                copy.wait_recv()
            total = r2[0]
            for k in range(1, ngy):
                total = total + r2[k]
            gfin[gx] = total
            made[:] = spread("gx", gx, ngx, lambda k, to: (gfin.at[gx], gfin.at[gx]), s3, v3)

        def last():
            for copy in made:
                copy.wait_recv()
            return gfin[...].reshape(value.shape)

        return second, third, last

    second_a, third_a, last_a = reduction(
        0, jnp.concatenate([g01, jnp.concatenate([g22, square], axis=1)], axis=0)
    )

    for h in range(PARTS):
        def next_image(x, y):
            fs[x, y, slice(h * half, (h + 1) * half), :] = image(fq, x, y, h)

        arrive_q[h]()
        each_cell(next_image)
    second_a()

    def final(i, carry):
        return carry + times(wide_of(fq, 1, i), wide_of(fs, 0, i))

    g33 = lax.fori_loop(0, steps, final, square)
    second_b, third_b, last_b = reduction(1, jnp.concatenate([g33, square], axis=1))
    third_a()
    second_b()
    whole = last_a()
    top, low = whole[:cols], whole[cols:]
    panels = cols // 8
    state = eliminate(tiles_of(top), tiles_of(low), cols, panels // 2)
    third_b()
    lead, rest = eliminate(*state, cols, panels - panels // 2)
    lead, rest = jnp.concatenate(lead, axis=0), jnp.concatenate(rest, axis=0)
    alpha = lead[:, cols:]
    inv2 = rest[:, :cols]
    g2, g1 = low[:, :cols], top[:, cols:]
    prod = jnp.dot(
        g2, jnp.concatenate([alpha, inv2], axis=1), precision=HI, preferred_element_type=F32
    )
    g3 = last_b()[:, :cols]
    system = jnp.concatenate([g1, g3], axis=1) - prod
    lead, _ = eliminate(tiles_of(system), [], cols, panels)
    c1 = jnp.concatenate(lead, axis=0)[:, cols:]
    c0 = alpha - jnp.dot(inv2, c1, precision=HI, preferred_element_type=F32)
    stacked = jnp.concatenate([c0, c1], axis=0)
    stacked = jnp.concatenate([stacked, jnp.zeros_like(stacked)], axis=1).T[:cols]
    ch, cl = split(stacked)
    factors = jnp.concatenate(
        [
            jnp.concatenate([ch, ch], axis=1),
            jnp.concatenate([cl, jnp.zeros_like(cl)], axis=1),
        ],
        axis=0,
    )

    def advance(x, y):
        def pair(buf):
            return jnp.concatenate([buf[x, y], buf[x, y + 1]], axis=1)

        hi, lo = split(jnp.concatenate([pair(fr), pair(fq)], axis=0))
        out = jnp.dot(factors, jnp.concatenate([hi, lo], axis=0), preferred_element_type=F32)
        out = out[:cols] + out[cols:]
        fx[x, y, :cols, :] = fx[x, y, :cols, :] + out[:, :128]
        fx[x, y + 1, :cols, :] = fx[x, y + 1, :cols, :] + out[:, 128:]

    for leave in leaves:
        leave()
    for x in range(1, cx + 1):
        for y in range(0, cy + 2, 2):
            advance(x, y)
    store = pltpu.make_async_copy(
        fx.at[pl.ds(1, cx), pl.ds(1, cy), pl.ds(0, cols)], x_out, local.at[0]
    )
    store.start()
    for x in (0, cx + 1):
        for y in range(1, cy + 1, 2):
            advance(x, y)

    arrive_l()

    def field(i, ys):
        return fx[i, ys, :cols, :], fl[i, ys, :, :]

    mid_y = slice(1, cy + 1)
    term_x = []
    for i in range(cx + 1):
        (u0, l0), (u1, l1) = field(i, mid_y), field(i + 1, mid_y)
        term_x.append(jnp.sum((u1 - u0) * (l1 - l0), axis=1))
    lane_y = lax.broadcasted_iota(jnp.int32, (cy, 128), 1)
    for i in range(cx):
        (u0, l0), (u1, l1) = field(i + 1, slice(0, cy + 1)), field(i + 1, slice(1, cy + 2))
        term_y = jnp.sum((u1 - u0) * (l1 - l0), axis=1)
        u, l = field(i + 1, mid_y)
        u, l = u.reshape(cy * cols, 128), l.reshape(cy * cols, 128)
        lane_f = lax.broadcasted_iota(jnp.int32, u.shape, 1)
        du = u - jnp.where(lane_f == 0, 0.0, pltpu.roll(u, 1, 1))
        dl = l - jnp.where(lane_f == 0, 0.0, pltpu.roll(l, 1, 1))
        term_z = jnp.sum((du * dl).reshape(cy, cols, 128), axis=1)
        end = jnp.sum((u * l).reshape(cy, cols, 128), axis=1)
        upper = jnp.where(lane_y == 127, end, pltpu.roll(term_z, 127, 1))
        gl[i] = (-0.5 / cols) * (
            term_x[i] + term_x[i + 1] + term_y[:-1] + term_y[1:] + term_z + upper
        )

    made = []
    for k in range(1, nsrc):
        copy = pltpu.make_async_remote_copy(
            src_ref=gl, dst_ref=gr.at[k - 1], send_sem=s4.at[k - 1], recv_sem=v4.at[k - 1],
            device_id=peer("src", lax.rem(src + k, nsrc)), device_id_type=MESH,
        )
        copy.start()
        made.append(copy)
    late.extend(made)
    summed = gl[...]
    for k, copy in enumerate(made):
        copy.wait_recv()
        summed = summed + gr[k]
    width = 128 // nsrc
    part = summed[:, :, :width]
    for k in range(1, nsrc):
        part = jnp.where(src == k, summed[:, :, k * width : (k + 1) * width], part)
    grad_out[...] = part
    store.wait()
    for copy in late:
        copy.wait_send()


def on_device(sizes, conductivity, electrodes, pair_order, initial_fields, adjoint_fields):
    ngx, ngy, nsrc = sizes
    cols, cx, cy, cz = initial_fields.shape
    pairs = electrodes.shape[0]
    dma = pltpu.SemaphoreType.DMA
    full = (cx + 2, cy + 2, cols, cz)
    rows = (2 * cols // ngx, cols // ngx)
    steps = 2 + 3 * PARTS
    x_out, grad = pl.pallas_call(
        functools.partial(kernel, (ngx, ngy, nsrc, cx, cy, cols)),
        out_shape=(
            jax.ShapeDtypeStruct((cx, cy, cols, cz), F32),
            jax.ShapeDtypeStruct((cx, cy, cz // nsrc), F32),
        ),
        in_specs=[pl.BlockSpec(memory_space=pltpu.HBM)] * 5,
        out_specs=(
            pl.BlockSpec(memory_space=pl.ANY),
            pl.BlockSpec(memory_space=pltpu.VMEM),
        ),
        scratch_shapes=[
            pltpu.VMEM((cx + 2, cy + 2, cols + 8, cz), F32),
            pltpu.VMEM(full, F32),
            pltpu.VMEM(full, F32),
            pltpu.VMEM(full, F32),
            pltpu.VMEM((cx, cy, cols, cz), F32),
            pltpu.VMEM((cx, cy, 7, 8, cz), F32),
            pltpu.VMEM((cx, cy, cz), F32),
            pltpu.VMEM((2, pairs), jnp.int32),
            pltpu.VMEM((1, cols), jnp.int32),
            pltpu.VMEM((2, cols, cz), jnp.int32),
            [pltpu.VMEM((ngx, n, 2 * cols), F32) for n in rows],
            [pltpu.VMEM((ngx - 1, n, 2 * cols), F32) for n in rows],
            [pltpu.VMEM((ngy, n, 2 * cols), F32) for n in rows],
            [pltpu.VMEM((ngx, n, 2 * cols), F32) for n in rows],
            pltpu.VMEM((cx, cy, cz), F32),
            pltpu.VMEM((nsrc - 1, cx, cy, cz), F32),
            dma((steps, 4)), dma((steps, 4)), dma((4 + PARTS,)),
            dma((2, ngx - 1)), dma((2, ngx - 1)),
            dma((2, ngy - 1)), dma((2, ngy - 1)),
            dma((2, ngx - 1)), dma((2, ngx - 1)),
            dma((nsrc - 1,)), dma((nsrc - 1,)),
        ],
        compiler_params=pltpu.CompilerParams(
            collective_id=0, has_side_effects=True, vmem_limit_bytes=62 * 1024 * 1024
        ),
        cost_estimate=pl.CostEstimate(
            flops=4 * 10**8, bytes_accessed=2 * 10**6, transcendentals=0
        ),
    )(
        conductivity, electrodes.T, pair_order.reshape(1, cols), initial_fields, adjoint_fields
    )
    return x_out.transpose(2, 0, 1, 3), grad


def solution(mesh):
    sizes = (mesh.shape["gx"], mesh.shape["gy"], mesh.shape["src"])
    field = P("src", "gx", "gy", None)
    return jax.shard_map(
        functools.partial(on_device, sizes),
        mesh=mesh,
        in_specs=(P("gx", "gy", None), P(), P("src"), field, field),
        out_specs=(field, P("gx", "gy", "src")),
        check_vma=False,
    )
```

time: 55 us -> 44.5 us (0.81)
  Pallas kernels: 47.8 us -> 40.9 us
  local copies, waits for them, and re-layouts: 6.02 us -> 2.75 us
    pallas_call x1, Pallas kernels: 47.8 us -> 40.9 us  [on_device(): pl.pallas_call(functools.partial(kernel, (ngx, ngy, nsrc, cx, cy, cols)),...]
    unnamed x12 -> x4, local copies, waits for them, and re-layouts: 5.94 us -> 2.75 us
where the time goes in v2:
time: 44.5 us; the launch traced here: 44.3 us
  Pallas kernels  40.9 us (92%)
  local copies, waits for them, and re-layouts  2.75 us (6%)
  between operations  0.65 us (1%)
    pallas_call x1, Pallas kernels, on_device(): pl.pallas_call(functools.partial(kernel, (ngx, ngy, nsrc, cx, cy, cols)),...  40.9 us
    unnamed x4, local copies, waits for them, and re-layouts  2.75 us

profile of v2, /device:TPU:0, one launch (start us, length us, event | category | flops | bytes accessed | tf_op | source)
XLA Modules:
  0.0 44.3 jit_solution(3243582879165928368)
XLA Ops:
  0.6 40.9 %shard_map.68 = (f32[2,8,64,128]{3,2,1,0:T(8,128)}, f32[2,8,64]{2,1,0:T(8,128)}) custom-call(f32[2,8,128]{2,1,0:T(8,128)} %sig_in.1, s32[2,128]{1,0:T(2,128)} %bitcast.4, s32[1,64]{1,0:T(1,128)} %bitcast.5, f32[64,2,8,128]{3,2,1,0:T(8,128)} %x_in.1, f32[64,2,8,128]{3,2,1,0:T(8,128)} %adj_in.1), custom_call_target="tpu_custom_call" | custom-call | flops 400000000 | bytes 2000000 | tf_op jit(solution)/shard_map/pallas_call | solution.py:456
  41.5 0.0 copy-start
  41.5 2.1 %copy.7 = f32[64,2,8,128]{3,2,1,0:T(8,128)} copy(f32[64,2,8,128]{3,0,2,1:T(8,128)} %bitcast.3) | data formatting | bytes 1048576
  43.7 0.0 copy-done
  43.7 0.6 %copy.9 = f32[2,8,64]{2,1,0:T(8,128)} copy(f32[2,8,64]{2,1,0:T(8,128)S(1)} %copy-done) | data formatting | bytes 8192
Async XLA Ops:
  41.5 2.2 %copy-start = (f32[2,8,64]{2,1,0:T(8,128)S(1)}, f32[2,8,64]{2,1,0:T(8,128)}, u32[]{:S(2)}) copy-start(f32[2,8,64]{2,1,0:T(8,128)} %get-tuple-element.11) | copy-start | bytes 12292

commit v3 on v2

--- a/solution.py
+++ b/solution.py
@@ -257,9 +257,6 @@
         each_cell(first)
         arrive_q.append(exchange(1 + 2 * PARTS + h, fq, h * half, half))
 
-    load_l.wait()
-    arrive_l = exchange(1 + 3 * PARTS, fl, 0, cols)
-
     def wide_of(buf, o, i):
         x, y = i // (cy // group), group * lax.rem(i, cy // group)
         return split(
@@ -349,6 +346,8 @@
     panels = cols // 8
     state = eliminate(tiles_of(top), tiles_of(low), cols, panels // 2)
     third_b()
+    load_l.wait()
+    arrive_l = exchange(1 + 3 * PARTS, fl, 0, cols)
     lead, rest = eliminate(*state, cols, panels - panels // 2)
     lead, rest = jnp.concatenate(lead, axis=0), jnp.concatenate(rest, axis=0)
     alpha = lead[:, cols:]
@@ -388,39 +387,45 @@
     for x in range(1, cx + 1):
         for y in range(0, cy + 2, 2):
             advance(x, y)
-    store = pltpu.make_async_copy(
-        fx.at[pl.ds(1, cx), pl.ds(1, cy), pl.ds(0, cols)], x_out, local.at[0]
-    )
-    store.start()
+            for row in (y, y + 1):
+                if 1 <= row <= cy:
+                    pltpu.make_async_copy(
+                        fx.at[x, row, pl.ds(0, cols)], x_out.at[:, x - 1, row - 1], local.at[0]
+                    ).start()
     for x in (0, cx + 1):
         for y in range(1, cy + 1, 2):
             advance(x, y)
 
     arrive_l()
 
-    def field(i, ys):
-        return fx[i, ys, :cols, :], fl[i, ys, :, :]
-
-    mid_y = slice(1, cy + 1)
-    term_x = []
-    for i in range(cx + 1):
-        (u0, l0), (u1, l1) = field(i, mid_y), field(i + 1, mid_y)
-        term_x.append(jnp.sum((u1 - u0) * (l1 - l0), axis=1))
-    lane_y = lax.broadcasted_iota(jnp.int32, (cy, 128), 1)
-    for i in range(cx):
-        (u0, l0), (u1, l1) = field(i + 1, slice(0, cy + 1)), field(i + 1, slice(1, cy + 2))
-        term_y = jnp.sum((u1 - u0) * (l1 - l0), axis=1)
-        u, l = field(i + 1, mid_y)
-        u, l = u.reshape(cy * cols, 128), l.reshape(cy * cols, 128)
-        lane_f = lax.broadcasted_iota(jnp.int32, u.shape, 1)
-        du = u - jnp.where(lane_f == 0, 0.0, pltpu.roll(u, 1, 1))
-        dl = l - jnp.where(lane_f == 0, 0.0, pltpu.roll(l, 1, 1))
-        term_z = jnp.sum((du * dl).reshape(cy, cols, 128), axis=1)
-        end = jnp.sum((u * l).reshape(cy, cols, 128), axis=1)
-        upper = jnp.where(lane_y == 127, end, pltpu.roll(term_z, 127, 1))
-        gl[i] = (-0.5 / cols) * (
-            term_x[i] + term_x[i + 1] + term_y[:-1] + term_y[1:] + term_z + upper
-        )
+    tall = (cols // 8, 8, 128)
+
+    def cell(x, y):
+        return fx[x, y, :cols, :], fl[x, y, :, :]
+
+    def rows_of(x):
+        return jnp.sum(x.reshape(tall), axis=0)
+
+    def face(x0, y0, x1, y1):
+        (u0, l0), (u1, l1) = cell(x0, y0), cell(x1, y1)
+        return rows_of((u1 - u0) * (l1 - l0))
+
+    lane_f = lax.broadcasted_iota(jnp.int32, (cols, 128), 1)
+    below = [face(0, y, 1, y) for y in range(1, cy + 1)]
+    for x in range(1, cx + 1):
+        left = face(x, 0, x, 1)
+        lines = []
+        for y in range(1, cy + 1):
+            above, right = face(x, y, x + 1, y), face(x, y, x, y + 1)
+            u, l = cell(x, y)
+            du = u - jnp.where(lane_f == 0, 0.0, pltpu.roll(u, 1, 1))
+            dl = l - jnp.where(lane_f == 0, 0.0, pltpu.roll(l, 1, 1))
+            term_z, end = rows_of(du * dl), rows_of(u * l)
+            upper = jnp.where(lane == 127, end, pltpu.roll(term_z, 127, 1))
+            total = (below[y - 1] + above) + (left + right) + (term_z + upper)
+            lines.append(jnp.sum(total, axis=0, keepdims=True))
+            below[y - 1], left = above, right
+        gl[x - 1] = (-0.5 / cols) * jnp.concatenate(lines, axis=0)
 
     made = []
     for k in range(1, nsrc):
@@ -440,7 +445,8 @@
     for k in range(1, nsrc):
         part = jnp.where(src == k, summed[:, :, k * width : (k + 1) * width], part)
     grad_out[...] = part
-    store.wait()
+    written = fx.at[pl.ds(1, cx), pl.ds(1, cy), pl.ds(0, cols)]
+    pltpu.make_async_copy(written, written, local.at[0]).wait()
     for copy in late:
         copy.wait_send()
 
@@ -453,10 +459,10 @@
     full = (cx + 2, cy + 2, cols, cz)
     rows = (2 * cols // ngx, cols // ngx)
     steps = 2 + 3 * PARTS
-    x_out, grad = pl.pallas_call(
+    return pl.pallas_call(
         functools.partial(kernel, (ngx, ngy, nsrc, cx, cy, cols)),
         out_shape=(
-            jax.ShapeDtypeStruct((cx, cy, cols, cz), F32),
+            jax.ShapeDtypeStruct((cols, cx, cy, cz), F32),
             jax.ShapeDtypeStruct((cx, cy, cz // nsrc), F32),
         ),
         in_specs=[pl.BlockSpec(memory_space=pltpu.HBM)] * 5,
@@ -496,7 +502,6 @@
     )(
         conductivity, electrodes.T, pair_order.reshape(1, cols), initial_fields, adjoint_fields
     )
-    return x_out.transpose(2, 0, 1, 3), grad
 
 
 def solution(mesh):

time: 44.5 us -> 41.6 us (0.935)
  Pallas kernels: 40.9 us -> 38.3 us
    pallas_call x1, Pallas kernels: 40.9 us -> 38.3 us  [on_device(): pl.pallas_call(functools.partial(kernel, (ngx, ngy, nsrc, cx, cy, cols)),...]
where the time goes in v3:
time: 41.6 us; the launch traced here: 41.4 us
  Pallas kernels  38.3 us (92%)
  local copies, waits for them, and re-layouts  2.48 us (6%)
  between operations  0.65 us (2%)
    pallas_call x1, Pallas kernels, on_device(): pl.pallas_call(functools.partial(kernel, (ngx, ngy, nsrc, cx, cy, cols)),...  38.3 us
    unnamed x4, local copies, waits for them, and re-layouts  2.48 us

profile of v3, /device:TPU:0, one launch (start us, length us, event | category | flops | bytes accessed | tf_op | source)
XLA Modules:
  0.0 41.4 jit_solution(12349157854040058959)
XLA Ops:
  0.6 38.3 %shard_map.68 = (f32[64,2,8,128]{3,2,1,0:T(8,128)}, f32[2,8,64]{2,1,0:T(8,128)}) custom-call(f32[2,8,128]{2,1,0:T(8,128)} %sig_in.1, s32[2,128]{1,0:T(2,128)} %bitcast.2, s32[1,64]{1,0:T(1,128)} %bitcast.3, f32[64,2,8,128]{3,2,1,0:T(8,128)} %x_in.1, f32[64,2,8,128]{3,2,1,0:T(8,128)} %adj_in.1), custom_call_target="tpu_custom_call" | custom-call | flops 400000000 | bytes 2000000 | tf_op jit(solution)/shard_map/pallas_call | solution.py:462
  38.9 0.0 copy-start
  38.9 1.9 %copy.9 = f32[64,2,8,128]{3,2,1,0:T(8,128)} copy(f32[64,2,8,128]{3,2,1,0:T(8,128)} %get-tuple-element.4) | data formatting | bytes 1048576
  40.8 0.0 copy-done
  40.8 0.6 %copy.10 = f32[2,8,64]{2,1,0:T(8,128)} copy(f32[2,8,64]{2,1,0:T(8,128)S(1)} %copy-done) | data formatting | bytes 8192
Async XLA Ops:
  38.9 1.9 %copy-start = (f32[2,8,64]{2,1,0:T(8,128)S(1)}, f32[2,8,64]{2,1,0:T(8,128)}, u32[]{:S(2)}) copy-start(f32[2,8,64]{2,1,0:T(8,128)} %get-tuple-element.5) | copy-start | bytes 12292

commit v4 on v3

--- a/solution.py
+++ b/solution.py
@@ -332,23 +332,26 @@
 
         arrive_q[h]()
         each_cell(next_image)
-    second_a()
+        if h == 0:
+            second_a()
+    third_a()
 
     def final(i, carry):
         return carry + times(wide_of(fq, 1, i), wide_of(fs, 0, i))
 
     g33 = lax.fori_loop(0, steps, final, square)
     second_b, third_b, last_b = reduction(1, jnp.concatenate([g33, square], axis=1))
-    third_a()
-    second_b()
     whole = last_a()
     top, low = whole[:cols], whole[cols:]
     panels = cols // 8
-    state = eliminate(tiles_of(top), tiles_of(low), cols, panels // 2)
+    third = panels // 3
+    state = eliminate(tiles_of(top), tiles_of(low), cols, third)
+    second_b()
+    state = eliminate(*state, cols, third)
     third_b()
     load_l.wait()
     arrive_l = exchange(1 + 3 * PARTS, fl, 0, cols)
-    lead, rest = eliminate(*state, cols, panels - panels // 2)
+    lead, rest = eliminate(*state, cols, panels - 2 * third)
     lead, rest = jnp.concatenate(lead, axis=0), jnp.concatenate(rest, axis=0)
     alpha = lead[:, cols:]
     inv2 = rest[:, :cols]
@@ -494,13 +497,19 @@
             dma((nsrc - 1,)), dma((nsrc - 1,)),
         ],
         compiler_params=pltpu.CompilerParams(
-            collective_id=0, has_side_effects=True, vmem_limit_bytes=62 * 1024 * 1024
+            collective_id=0, has_side_effects=True, vmem_limit_bytes=32 * 1024 * 1024
         ),
         cost_estimate=pl.CostEstimate(
             flops=4 * 10**8, bytes_accessed=2 * 10**6, transcendentals=0
         ),
     )(
-        conductivity, electrodes.T, pair_order.reshape(1, cols), initial_fields, adjoint_fields
+        *[
+            pltpu.with_memory_space_constraint(value, pltpu.HBM)
+            for value in (
+                conductivity, electrodes.T, pair_order.reshape(1, cols),
+                initial_fields, adjoint_fields,
+            )
+        ]
     )
 
 

time: 41.6 us -> 46.1 us (1.11)
  Pallas kernels: 38.3 us -> 43.9 us
  local copies, waits for them, and re-layouts: 2.48 us -> 1.39 us
    pallas_call x1, Pallas kernels: 38.3 us -> 43.9 us  [on_device(): pl.pallas_call(functools.partial(kernel, (ngx, ngy, nsrc, cx, cy, cols)),...]
    unnamed x4 -> x2, local copies, waits for them, and re-layouts: 2.48 us -> 1.39 us
where the time goes in v4:
time: 46.1 us; the launch traced here: 45.9 us
  Pallas kernels  43.9 us (95%)
  local copies, waits for them, and re-layouts  1.39 us (3%)
  between operations  0.64 us (1%)
    pallas_call x1, Pallas kernels, on_device(): pl.pallas_call(functools.partial(kernel, (ngx, ngy, nsrc, cx, cy, cols)),...  43.9 us
    unnamed x2, local copies, waits for them, and re-layouts  1.39 us

profile of v4, /device:TPU:0, one launch (start us, length us, event | category | flops | bytes accessed | tf_op | source)
XLA Modules:
  0.0 45.9 jit_solution(7481812666342515134)
XLA Ops:
  0.6 43.9 %shard_map.68 = (f32[64,2,8,128]{3,2,1,0:T(8,128)S(1)}, f32[2,8,64]{2,1,0:T(8,128)S(1)}) custom-call(f32[2,8,128]{2,1,0:T(8,128)} %sig_in.1, s32[2,128]{1,0:T(2,128)} %bitcast.2, s32[1,64]{1,0:T(1,128)} %bitcast.3, f32[64,2,8,128]{3,2,1,0:T(8,128)} %x_in.1, f32[64,2,8,128]{3,2,1,0:T(8,128)} %adj_in.1), custom_call_target="tpu_custom_call" | custom-call | flops 400000000 | bytes 2000000 | tf_op jit(solution)/shard_map/pallas_call | solution.py:465
  44.5 0.8 %copy.9 = f32[64,2,8,128]{3,2,1,0:T(8,128)} copy(f32[64,2,8,128]{3,2,1,0:T(8,128)S(1)} %get-tuple-element.4) | data formatting | bytes 1048576
  45.3 0.6 %copy.10 = f32[2,8,64]{2,1,0:T(8,128)} copy(f32[2,8,64]{2,1,0:T(8,128)S(1)} %get-tuple-element.5) | data formatting | bytes 8192

commit v5 on v4

--- a/solution.py
+++ b/solution.py
@@ -382,19 +382,17 @@
         hi, lo = split(jnp.concatenate([pair(fr), pair(fq)], axis=0))
         out = jnp.dot(factors, jnp.concatenate([hi, lo], axis=0), preferred_element_type=F32)
         out = out[:cols] + out[cols:]
-        fx[x, y, :cols, :] = fx[x, y, :cols, :] + out[:, :128]
-        fx[x, y + 1, :cols, :] = fx[x, y + 1, :cols, :] + out[:, 128:]
+        for k in range(2):
+            new = fx[x, y + k, :cols, :] + out[:, 128 * k : 128 * (k + 1)]
+            fx[x, y + k, :cols, :] = new
+            if 1 <= x <= cx and 1 <= y + k <= cy:
+                x_out[x - 1, y + k - 1] = new
 
     for leave in leaves:
         leave()
     for x in range(1, cx + 1):
         for y in range(0, cy + 2, 2):
             advance(x, y)
-            for row in (y, y + 1):
-                if 1 <= row <= cy:
-                    pltpu.make_async_copy(
-                        fx.at[x, row, pl.ds(0, cols)], x_out.at[:, x - 1, row - 1], local.at[0]
-                    ).start()
     for x in (0, cx + 1):
         for y in range(1, cy + 1, 2):
             advance(x, y)
@@ -448,8 +446,6 @@
     for k in range(1, nsrc):
         part = jnp.where(src == k, summed[:, :, k * width : (k + 1) * width], part)
     grad_out[...] = part
-    written = fx.at[pl.ds(1, cx), pl.ds(1, cy), pl.ds(0, cols)]
-    pltpu.make_async_copy(written, written, local.at[0]).wait()
     for copy in late:
         copy.wait_send()
 
@@ -462,17 +458,14 @@
     full = (cx + 2, cy + 2, cols, cz)
     rows = (2 * cols // ngx, cols // ngx)
     steps = 2 + 3 * PARTS
-    return pl.pallas_call(
+    x_out, grad = pl.pallas_call(
         functools.partial(kernel, (ngx, ngy, nsrc, cx, cy, cols)),
         out_shape=(
-            jax.ShapeDtypeStruct((cols, cx, cy, cz), F32),
+            jax.ShapeDtypeStruct((cx, cy, cols, cz), F32),
             jax.ShapeDtypeStruct((cx, cy, cz // nsrc), F32),
         ),
         in_specs=[pl.BlockSpec(memory_space=pltpu.HBM)] * 5,
-        out_specs=(
-            pl.BlockSpec(memory_space=pl.ANY),
-            pl.BlockSpec(memory_space=pltpu.VMEM),
-        ),
+        out_specs=(pl.BlockSpec(memory_space=pltpu.VMEM),) * 2,
         scratch_shapes=[
             pltpu.VMEM((cx + 2, cy + 2, cols + 8, cz), F32),
             pltpu.VMEM(full, F32),
@@ -511,6 +504,7 @@
             )
         ]
     )
+    return x_out.transpose(2, 0, 1, 3), grad
 
 
 def solution(mesh):

time: 46.1 us -> 44.5 us (0.965)
  Pallas kernels: 43.9 us -> 41.9 us
    pallas_call x1, Pallas kernels: 43.9 us -> 41.9 us  [on_device(): pl.pallas_call(functools.partial(kernel, (ngx, ngy, nsrc, cx, cy, cols)),...]
where the time goes in v5:
time: 44.5 us; the launch traced here: 44.3 us
  Pallas kernels  41.9 us (94%)
  local copies, waits for them, and re-layouts  1.7 us (4%)
  between operations  0.64 us (1%)
    pallas_call x1, Pallas kernels, on_device(): pl.pallas_call(functools.partial(kernel, (ngx, ngy, nsrc, cx, cy, cols)),...  41.9 us
    unnamed x2, local copies, waits for them, and re-layouts  1.7 us

profile of v5, /device:TPU:0, one launch (start us, length us, event | category | flops | bytes accessed | tf_op | source)
XLA Modules:
  0.0 44.3 jit_solution(4741906215751938238)
XLA Ops:
  0.6 41.9 %shard_map.68 = (f32[2,8,64,128]{3,2,1,0:T(8,128)S(1)}, f32[2,8,64]{2,1,0:T(8,128)S(1)}) custom-call(f32[2,8,128]{2,1,0:T(8,128)} %sig_in.1, s32[2,128]{1,0:T(2,128)} %bitcast.4, s32[1,64]{1,0:T(1,128)} %bitcast.5, f32[64,2,8,128]{3,2,1,0:T(8,128)} %x_in.1, f32[64,2,8,128]{3,2,1,0:T(8,128)} %adj_in.1), custom_call_target="tpu_custom_call" | custom-call | flops 400000000 | bytes 2000000 | tf_op jit(solution)/shard_map/pallas_call | solution.py:461
  42.6 1.1 %copy.7 = f32[64,2,8,128]{3,2,1,0:T(8,128)} copy(f32[64,2,8,128]{3,0,2,1:T(8,128)S(1)} %bitcast.3) | data formatting | bytes 1048576
  43.7 0.6 %copy.9 = f32[2,8,64]{2,1,0:T(8,128)} copy(f32[2,8,64]{2,1,0:T(8,128)S(1)} %get-tuple-element.11) | data formatting | bytes 8192

commit v6 on v5

--- a/solution.py
+++ b/solution.py
@@ -332,26 +332,21 @@
 
         arrive_q[h]()
         each_cell(next_image)
-        if h == 0:
-            second_a()
-    third_a()
+    second_a()
 
     def final(i, carry):
         return carry + times(wide_of(fq, 1, i), wide_of(fs, 0, i))
 
     g33 = lax.fori_loop(0, steps, final, square)
     second_b, third_b, last_b = reduction(1, jnp.concatenate([g33, square], axis=1))
+    third_a()
+    second_b()
     whole = last_a()
     top, low = whole[:cols], whole[cols:]
     panels = cols // 8
-    third = panels // 3
-    state = eliminate(tiles_of(top), tiles_of(low), cols, third)
-    second_b()
-    state = eliminate(*state, cols, third)
+    state = eliminate(tiles_of(top), tiles_of(low), cols, panels // 2)
     third_b()
-    load_l.wait()
-    arrive_l = exchange(1 + 3 * PARTS, fl, 0, cols)
-    lead, rest = eliminate(*state, cols, panels - 2 * third)
+    lead, rest = eliminate(*state, cols, panels - panels // 2)
     lead, rest = jnp.concatenate(lead, axis=0), jnp.concatenate(rest, axis=0)
     alpha = lead[:, cols:]
     inv2 = rest[:, :cols]
@@ -360,6 +355,8 @@
         g2, jnp.concatenate([alpha, inv2], axis=1), precision=HI, preferred_element_type=F32
     )
     g3 = last_b()[:, :cols]
+    load_l.wait()
+    arrive_l = exchange(1 + 3 * PARTS, fl, 0, cols)
     system = jnp.concatenate([g1, g3], axis=1) - prod
     lead, _ = eliminate(tiles_of(system), [], cols, panels)
     c1 = jnp.concatenate(lead, axis=0)[:, cols:]

time: 44.5 us -> 41.5 us (0.933)
  the two profiles are of different devices: /device:TPU:0 before, /device:TPU:1 now
where the time goes in v6:
time: 41.5 us; the launch traced here: 41.3 us
  Pallas kernels  39 us (94%)
  local copies, waits for them, and re-layouts  1.7 us (4%)
  between operations  0.64 us (2%)
    pallas_call x1, Pallas kernels, on_device(): pl.pallas_call(functools.partial(kernel, (ngx, ngy, nsrc, cx, cy, cols)),...  39 us
    unnamed x2, local copies, waits for them, and re-layouts  1.7 us

profile of v6, /device:TPU:1, one launch (start us, length us, event | category | flops | bytes accessed | tf_op | source)
XLA Modules:
  0.0 41.3 jit_solution(14498472558221371173)
XLA Ops:
  0.6 39.0 %shard_map.68 = (f32[2,8,64,128]{3,2,1,0:T(8,128)S(1)}, f32[2,8,64]{2,1,0:T(8,128)S(1)}) custom-call(f32[2,8,128]{2,1,0:T(8,128)} %sig_in.1, s32[2,128]{1,0:T(2,128)} %bitcast.4, s32[1,64]{1,0:T(1,128)} %bitcast.5, f32[64,2,8,128]{3,2,1,0:T(8,128)} %x_in.1, f32[64,2,8,128]{3,2,1,0:T(8,128)} %adj_in.1), custom_call_target="tpu_custom_call" | custom-call | flops 400000000 | bytes 2000000 | tf_op jit(solution)/shard_map/pallas_call | solution.py:458
  39.6 1.1 %copy.7 = f32[64,2,8,128]{3,2,1,0:T(8,128)} copy(f32[64,2,8,128]{3,0,2,1:T(8,128)S(1)} %bitcast.3) | data formatting | bytes 1048576
  40.7 0.6 %copy.9 = f32[2,8,64]{2,1,0:T(8,128)} copy(f32[2,8,64]{2,1,0:T(8,128)S(1)} %get-tuple-element.11) | data formatting | bytes 8192

commit v7 on v6

--- a/solution.py
+++ b/solution.py
@@ -346,6 +346,8 @@
     panels = cols // 8
     state = eliminate(tiles_of(top), tiles_of(low), cols, panels // 2)
     third_b()
+    load_l.wait()
+    arrive_l = exchange(1 + 3 * PARTS, fl, 0, cols)
     lead, rest = eliminate(*state, cols, panels - panels // 2)
     lead, rest = jnp.concatenate(lead, axis=0), jnp.concatenate(rest, axis=0)
     alpha = lead[:, cols:]
@@ -355,8 +357,6 @@
         g2, jnp.concatenate([alpha, inv2], axis=1), precision=HI, preferred_element_type=F32
     )
     g3 = last_b()[:, :cols]
-    load_l.wait()
-    arrive_l = exchange(1 + 3 * PARTS, fl, 0, cols)
     system = jnp.concatenate([g1, g3], axis=1) - prod
     lead, _ = eliminate(tiles_of(system), [], cols, panels)
     c1 = jnp.concatenate(lead, axis=0)[:, cols:]

time: 41.5 us -> 40.2 us (0.969)
  the two profiles are of different devices: /device:TPU:1 before, /device:TPU:0 now
where the time goes in v7:
time: 40.2 us; the launch traced here: 40 us
  Pallas kernels  37.7 us (94%)
  local copies, waits for them, and re-layouts  1.7 us (4%)
  between operations  0.64 us (2%)
    pallas_call x1, Pallas kernels, on_device(): pl.pallas_call(functools.partial(kernel, (ngx, ngy, nsrc, cx, cy, cols)),...  37.7 us
    unnamed x2, local copies, waits for them, and re-layouts  1.7 us

profile of v7, /device:TPU:0, one launch (start us, length us, event | category | flops | bytes accessed | tf_op | source)
XLA Modules:
  0.0 40.0 jit_solution(6898221487369814918)
XLA Ops:
  0.6 37.7 %shard_map.68 = (f32[2,8,64,128]{3,2,1,0:T(8,128)S(1)}, f32[2,8,64]{2,1,0:T(8,128)S(1)}) custom-call(f32[2,8,128]{2,1,0:T(8,128)} %sig_in.1, s32[2,128]{1,0:T(2,128)} %bitcast.4, s32[1,64]{1,0:T(1,128)} %bitcast.5, f32[64,2,8,128]{3,2,1,0:T(8,128)} %x_in.1, f32[64,2,8,128]{3,2,1,0:T(8,128)} %adj_in.1), custom_call_target="tpu_custom_call" | custom-call | flops 400000000 | bytes 2000000 | tf_op jit(solution)/shard_map/pallas_call | solution.py:458
  38.3 1.1 %copy.7 = f32[64,2,8,128]{3,2,1,0:T(8,128)} copy(f32[64,2,8,128]{3,0,2,1:T(8,128)S(1)} %bitcast.3) | data formatting | bytes 1048576
  39.4 0.6 %copy.9 = f32[2,8,64]{2,1,0:T(8,128)} copy(f32[2,8,64]{2,1,0:T(8,128)S(1)} %get-tuple-element.11) | data formatting | bytes 8192

commit v8 on v7

--- a/solution.py
+++ b/solution.py
@@ -69,7 +69,7 @@
     return [x[8 * t : 8 * t + 8] for t in range(x.shape[0] // 8)]
 
 
-PARTS = 2
+PARTS = 4
 
 
 def kernel(
@@ -182,14 +182,16 @@
 
     group = 4
 
+    bunch = cy
+
     def each_cell(body):
         def step(i, carry):
-            x, y = i // (cy // group), group * lax.rem(i, cy // group)
-            for k in range(group):
+            x, y = i // (cy // bunch), bunch * lax.rem(i, cy // bunch)
+            for k in range(bunch):
                 body(x, y + k)
             return carry
 
-        lax.fori_loop(0, cx * cy // group, step, 0)
+        lax.fori_loop(0, cx * cy // bunch, step, 0)
 
     def conductance(x, y):
         def sig_at(i, j):

time: 40.2 us -> 39.7 us (0.988)
  Pallas kernels: 37.7 us -> 37.1 us
    pallas_call x1, Pallas kernels: 37.7 us -> 37.1 us  [on_device(): pl.pallas_call(functools.partial(kernel, (ngx, ngy, nsrc, cx, cy, cols)),...]
where the time goes in v8:
time: 39.7 us; the launch traced here: 39.5 us
  Pallas kernels  37.1 us (93%)
  local copies, waits for them, and re-layouts  1.7 us (4%)
  between operations  0.64 us (2%)
    pallas_call x1, Pallas kernels, on_device(): pl.pallas_call(functools.partial(kernel, (ngx, ngy, nsrc, cx, cy, cols)),...  37.1 us
    unnamed x2, local copies, waits for them, and re-layouts  1.7 us

profile of v8, /device:TPU:0, one launch (start us, length us, event | category | flops | bytes accessed | tf_op | source)
XLA Modules:
  0.0 39.5 jit_solution(154483037404071642)
XLA Ops:
  0.6 37.1 %shard_map.68 = (f32[2,8,64,128]{3,2,1,0:T(8,128)S(1)}, f32[2,8,64]{2,1,0:T(8,128)S(1)}) custom-call(f32[2,8,128]{2,1,0:T(8,128)} %sig_in.1, s32[2,128]{1,0:T(2,128)} %bitcast.4, s32[1,64]{1,0:T(1,128)} %bitcast.5, f32[64,2,8,128]{3,2,1,0:T(8,128)} %x_in.1, f32[64,2,8,128]{3,2,1,0:T(8,128)} %adj_in.1), custom_call_target="tpu_custom_call" | custom-call | flops 400000000 | bytes 2000000 | tf_op jit(solution)/shard_map/pallas_call | solution.py:460
  37.8 1.1 %copy.7 = f32[64,2,8,128]{3,2,1,0:T(8,128)} copy(f32[64,2,8,128]{3,0,2,1:T(8,128)S(1)} %bitcast.3) | data formatting | bytes 1048576
  38.9 0.6 %copy.9 = f32[2,8,64]{2,1,0:T(8,128)} copy(f32[2,8,64]{2,1,0:T(8,128)S(1)} %get-tuple-element.11) | data formatting | bytes 8192

commit v9 on v8

--- a/solution.py
+++ b/solution.py
@@ -62,7 +62,10 @@
             rest = rest[1:] + rest[:1]
         return tuple(lead), tuple(rest)
 
-    return lax.fori_loop(0, panels, panel, (tuple(lead), tuple(rest)))
+    def pair(step, carry):
+        return panel(step, panel(step, carry))
+
+    return lax.fori_loop(0, panels // 2, pair, (tuple(lead), tuple(rest)))
 
 
 def tiles_of(x):

time: 39.7 us -> 40 us (level)
  no operation moved by 1% of the time
where the time goes in v9:
time: 40 us; the launch traced here: 39.8 us
  Pallas kernels  37.4 us (94%)
  local copies, waits for them, and re-layouts  1.7 us (4%)
  between operations  0.64 us (2%)
    pallas_call x1, Pallas kernels, on_device(): pl.pallas_call(functools.partial(kernel, (ngx, ngy, nsrc, cx, cy, cols)),...  37.4 us
    unnamed x2, local copies, waits for them, and re-layouts  1.7 us

profile of v9, /device:TPU:0, one launch (start us, length us, event | category | flops | bytes accessed | tf_op | source)
XLA Modules:
  0.0 39.8 jit_solution(6375392540968516407)
XLA Ops:
  0.6 37.4 %shard_map.68 = (f32[2,8,64,128]{3,2,1,0:T(8,128)S(1)}, f32[2,8,64]{2,1,0:T(8,128)S(1)}) custom-call(f32[2,8,128]{2,1,0:T(8,128)} %sig_in.1, s32[2,128]{1,0:T(2,128)} %bitcast.4, s32[1,64]{1,0:T(1,128)} %bitcast.5, f32[64,2,8,128]{3,2,1,0:T(8,128)} %x_in.1, f32[64,2,8,128]{3,2,1,0:T(8,128)} %adj_in.1), custom_call_target="tpu_custom_call" | custom-call | flops 400000000 | bytes 2000000 | tf_op jit(solution)/shard_map/pallas_call | solution.py:463
  38.1 1.1 %copy.7 = f32[64,2,8,128]{3,2,1,0:T(8,128)} copy(f32[64,2,8,128]{3,0,2,1:T(8,128)S(1)} %bitcast.3) | data formatting | bytes 1048576
  39.2 0.6 %copy.9 = f32[2,8,64]{2,1,0:T(8,128)} copy(f32[2,8,64]{2,1,0:T(8,128)S(1)} %get-tuple-element.11) | data formatting | bytes 8192
